TPU v7x, 32 devices: a whole 2x2x4 slice. The times are simulated.
32 devices in a mesh: dp: 8 (over z, y), tensor: 4 (over x, core).
Axes of the slice: x: 2, y: 2, z: 4, core: 2. Of those that a mesh axis runs over, the one named last changes fastest.
Arguments:
- tokens: bfloat16 [24576, 768], P(('dp', 'tensor')), may hold values from -6 to 6
- cotangent: bfloat16 [24576, 768], P(('dp', 'tensor')), may hold values from -4.5 to 4.5
- segment_ids: int32 [24576], P('dp'), may hold values from 0 to 15, as said below
- valid: int32 [24576], P(('dp', 'tensor')), may hold values from 0 to 1, as said below
- qkv_weight: float32 [768, 3, 768], P('dp', None, 'tensor'), may hold values from -0.21875 to 0.21875
- qkv_moment1: float32 [768, 3, 768], P('dp', None, 'tensor'), may hold values from -0.0015025384 to 0.0015025384
- qkv_moment2: float32 [768, 3, 768], P('dp', None, 'tensor'), may hold values from 1.4110135e-07 to 5.644054e-07
- out_weight: float32 [768, 768], P('tensor', 'dp'), may hold values from -0.649519 to 0.649519
- out_moment1: float32 [768, 768], P('tensor', 'dp'), may hold values from -0.0015025384 to 0.0015025384
- out_moment2: float32 [768, 768], P('tensor', 'dp'), may hold values from 1.4110135e-07 to 5.644054e-07
- fc_weight: float32 [768, 3072], P('dp', 'tensor'), may hold values from -0.21875 to 0.21875
- fc_moment1: float32 [768, 3072], P('dp', 'tensor'), may hold values from -0.0015025384 to 0.0015025384
- fc_moment2: float32 [768, 3072], P('dp', 'tensor'), may hold values from 1.4110135e-07 to 5.644054e-07
- proj_weight: float32 [3072, 768], P('tensor', 'dp'), may hold values from -0.16237976 to 0.16237976
- proj_moment1: float32 [3072, 768], P('tensor', 'dp'), may hold values from -0.0015025384 to 0.0015025384
- proj_moment2: float32 [3072, 768], P('tensor', 'dp'), may hold values from 1.4110135e-07 to 5.644054e-07
- vector_params: float32 [8, 768], replicated, may hold values from -0.6 to 2.5
- vector_moment1: float32 [8, 768], replicated, may hold values from -0.0015025384 to 0.0015025384
- vector_moment2: float32 [8, 768], replicated, may hold values from 1.4110135e-07 to 5.644054e-07
- fc_bias: float32 [3072], replicated, may hold values from -0.6 to 0.6
- fc_bias_moment1: float32 [3072], replicated, may hold values from -0.0015025384 to 0.0015025384
- fc_bias_moment2: float32 [3072], replicated, may hold values from 1.4110135e-07 to 5.644054e-07
Outputs:
- mixed: bfloat16 [24576, 768], P(('dp', 'tensor'))
- input_grad: bfloat16 [24576, 768], P(('dp', 'tensor'))
- grad_norm: float32 [], replicated
- qkv_weight_new: float32 [768, 3, 768], P('dp', None, 'tensor')
- qkv_moment1_new: float32 [768, 3, 768], P('dp', None, 'tensor')
- qkv_moment2_new: float32 [768, 3, 768], P('dp', None, 'tensor')
- out_weight_new: float32 [768, 768], P('tensor', 'dp')
- out_moment1_new: float32 [768, 768], P('tensor', 'dp')
- out_moment2_new: float32 [768, 768], P('tensor', 'dp')
- fc_weight_new: float32 [768, 3072], P('dp', 'tensor')
- fc_moment1_new: float32 [768, 3072], P('dp', 'tensor')
- fc_moment2_new: float32 [768, 3072], P('dp', 'tensor')
- proj_weight_new: float32 [3072, 768], P('tensor', 'dp')
- proj_moment1_new: float32 [3072, 768], P('tensor', 'dp')
- proj_moment2_new: float32 [3072, 768], P('tensor', 'dp')
- vector_params_new: float32 [8, 768], replicated
- vector_moment1_new: float32 [8, 768], replicated
- vector_moment2_new: float32 [8, 768], replicated
- fc_bias_new: float32 [3072], replicated
- fc_bias_moment1_new: float32 [3072], replicated
- fc_bias_moment2_new: float32 [3072], replicated
Inputs may be any that keep to these rules, and one draw needn't show every extreme that they name: `segment_ids`: rows of 1024 slots follow one another. Within a row the ids start at 0 and rise by one at each new sequence; a sequence has 64 to 1023 tokens; the slots whose valid is 0 end the row and share one id. Some row holds 16 sequences. `valid`: 1 on the slots of a row before its padding, 0 on the padding.
All inputs are finite; a program needn't handle non-finite values.
Results may differ from a plain program's by a relative error of at most 0.019.
Values may be sent and summed in bfloat16 or wider, within the bound.
A program may use at most 192 MiB of HBM per device.

v0:
```python
import math

import jax
import jax.numpy as jnp
from jax import lax
from jax.sharding import PartitionSpec as P

HD = 64
SLOT = 1024
STEP = 10


NORM_EPSILON = 1e-05
MASK_FILL = -1e30
DECAY_FIRST = 0.5
DECAY_SECOND = 0.5
ADAM_EPSILON = 1e-08
WEIGHT_DECAY = 0.1
CLIP_NORM = 1.0
RATE_MATRIX = 0.04
RATE_VECTOR = 0.3


def cut_along(shard, dim, devices):
    before, after = (shard.shape[:dim], shard.shape[dim + 1 :])
    return jnp.moveaxis(shard.reshape(*before, devices, -1, *after), dim, 0)


def sum_at_owner(shard, axis, dim):
    devices = lax.axis_size(axis)
    pieces = lax.all_to_all(cut_along(shard, dim, devices), axis, 0, 0, tiled=True)
    return jnp.sum(pieces.astype(jnp.float32), axis=0)


def layer_norm(values, gain_vector, shift_vector):
    centered = values - jnp.mean(values, axis=-1, keepdims=True)
    variance = jnp.mean(centered * centered, axis=-1, keepdims=True)
    return centered * lax.rsqrt(variance + NORM_EPSILON) * gain_vector + shift_vector


def gelu_tanh(values):
    return jax.nn.gelu(values, approximate=True)


def adamw_update(weight, moment_one, moment_two, gradient, step_rate, decay_rate):
    first_moment = DECAY_FIRST * moment_one + (1.0 - DECAY_FIRST) * gradient
    second_moment = DECAY_SECOND * moment_two + (1.0 - DECAY_SECOND) * gradient * gradient
    first_hat = first_moment / (1.0 - DECAY_FIRST**STEP)
    second_hat = second_moment / (1.0 - DECAY_SECOND**STEP)
    fresh_weight = weight - step_rate * (
        first_hat / (jnp.sqrt(second_hat) + ADAM_EPSILON) + decay_rate * weight
    )
    return (fresh_weight, first_moment, second_moment)


def masked_scores(query_rows, key_rows, segment_block, score_scale):
    places = jnp.arange(segment_block.shape[0])
    row_number = places // SLOT
    allowed = (
        (segment_block[:, None] == segment_block[None, :])
        & (row_number[:, None] == row_number[None, :])
        & (places[None, :] <= places[:, None])
    )
    scores = (
        jnp.einsum("qhe,khe->hqk", query_rows, key_rows, preferred_element_type=jnp.float32)
        * score_scale
    )
    return jnp.where(allowed[None], scores, MASK_FILL)


def on_device(
    tokens,
    cotangent,
    segment_ids,
    valid,
    qkv_weight,
    qkv_moment1,
    qkv_moment2,
    out_weight,
    out_moment1,
    out_moment2,
    fc_weight,
    fc_moment1,
    fc_moment2,
    proj_weight,
    proj_moment1,
    proj_moment2,
    vector_params,
    vector_moment1,
    vector_moment2,
    fc_bias,
    fc_bias_moment1,
    fc_bias_moment2,
):
    tensor_count = lax.axis_size("tensor")
    tensor_rank = lax.axis_index("tensor")
    model_width = vector_params.shape[1]
    local_width = model_width // tensor_count
    hidden_width = fc_bias.shape[0]
    local_hidden = hidden_width // tensor_count
    local_heads = local_width // HD
    group_rows = segment_ids.shape[0]
    block_rows = SLOT * math.gcd(group_rows // SLOT, max(1, 1024 // SLOT))
    block_count = group_rows // block_rows
    score_scale = float(HD) ** (-0.5)
    qkv_local, out_local, fc_local, proj_local = (
        lax.all_gather(qkv_weight.astype(jnp.bfloat16), "dp", axis=0, tiled=True),
        lax.all_gather(out_weight.astype(jnp.bfloat16), "dp", axis=1, tiled=True),
        lax.all_gather(fc_weight.astype(jnp.bfloat16), "dp", axis=0, tiled=True),
        lax.all_gather(proj_weight.astype(jnp.bfloat16), "dp", axis=1, tiled=True),
    )
    qkv_flat = qkv_local.reshape(model_width, 3 * local_width)
    column_start = tensor_rank * local_width
    hidden_start = tensor_rank * local_hidden
    query_bias = lax.dynamic_slice_in_dim(vector_params[4], column_start, local_width)
    value_bias = lax.dynamic_slice_in_dim(vector_params[5], column_start, local_width)
    fc_bias_local = lax.dynamic_slice_in_dim(fc_bias, hidden_start, local_hidden)

    def split_heads(rows_in):
        return rows_in.reshape(block_count, block_rows, local_heads, HD)

    def attend(bundle):
        query_rows, key_rows, value_rows, segment_block = bundle
        scores = masked_scores(query_rows, key_rows, segment_block, score_scale)
        top_score = jnp.max(scores, axis=-1, keepdims=True)
        exp_scores = jnp.exp(scores - top_score)
        exp_total = jnp.sum(exp_scores, axis=-1, keepdims=True)
        prob_low = (exp_scores / exp_total).astype(jnp.bfloat16)
        attended = jnp.einsum(
            "hqk,khe->qhe", prob_low, value_rows, preferred_element_type=jnp.float32
        )
        return (attended, top_score + jnp.log(exp_total))

    def attend_back(bundle):
        query_rows, key_rows, value_rows, segment_block, log_total, dcontext_rows = bundle
        scores = masked_scores(query_rows, key_rows, segment_block, score_scale)
        probs = jnp.exp(scores - log_total)
        grad_prob = jnp.einsum(
            "qhe,khe->hqk", dcontext_rows, value_rows, preferred_element_type=jnp.float32
        )
        inner_sum = jnp.sum(probs * grad_prob, axis=-1, keepdims=True)
        grad_score = (probs * (grad_prob - inner_sum)).astype(jnp.bfloat16)
        grad_query = (
            jnp.einsum("hqk,khe->qhe", grad_score, key_rows, preferred_element_type=jnp.float32)
            * score_scale
        )
        grad_key = (
            jnp.einsum("hqk,qhe->khe", grad_score, query_rows, preferred_element_type=jnp.float32)
            * score_scale
        )
        grad_value = jnp.einsum(
            "hqk,qhe->khe",
            probs.astype(jnp.bfloat16),
            dcontext_rows,
            preferred_element_type=jnp.float32,
        )
        return (grad_query, grad_key, grad_value)

    inputs = tokens.astype(jnp.float32)
    normed_one = layer_norm(inputs, vector_params[0], vector_params[1]).astype(jnp.bfloat16)
    normed_rows = lax.all_gather(normed_one, "tensor", axis=0, tiled=True)
    mixed_qkv = jnp.dot(normed_rows, qkv_flat, preferred_element_type=jnp.float32)
    query_all = (mixed_qkv[:, :local_width] + query_bias).astype(jnp.bfloat16)
    key_all = mixed_qkv[:, local_width : 2 * local_width].astype(jnp.bfloat16)
    value_all = (mixed_qkv[:, 2 * local_width :] + value_bias).astype(jnp.bfloat16)
    segment_blocks = segment_ids.reshape(block_count, block_rows)
    attended, log_totals = lax.map(
        attend,
        (split_heads(query_all), split_heads(key_all), split_heads(value_all), segment_blocks),
    )
    context = attended.reshape(group_rows, local_width).astype(jnp.bfloat16)
    attn_sum = lax.psum_scatter(
        jnp.dot(context, out_local, preferred_element_type=jnp.float32).astype(jnp.bfloat16),
        "tensor",
        scatter_dimension=0,
        tiled=True,
    ).astype(jnp.float32)
    resid = inputs + attn_sum + vector_params[6]
    normed_two = layer_norm(resid, vector_params[2], vector_params[3]).astype(jnp.bfloat16)
    normed_two_rows = lax.all_gather(normed_two, "tensor", axis=0, tiled=True)
    pre_act = jnp.dot(normed_two_rows, fc_local, preferred_element_type=jnp.float32) + fc_bias_local
    activated = gelu_tanh(pre_act).astype(jnp.bfloat16)
    branch_out = lax.psum_scatter(
        jnp.dot(activated, proj_local, preferred_element_type=jnp.float32).astype(jnp.bfloat16),
        "tensor",
        scatter_dimension=0,
        tiled=True,
    ).astype(jnp.float32)
    result = resid + branch_out + vector_params[7]
    mixed = result.astype(jnp.bfloat16)
    grad_out = cotangent.astype(jnp.float32) * valid.astype(jnp.float32)[:, None]
    proj_bias_grad = jnp.sum(grad_out, axis=0)
    grad_low = grad_out.astype(jnp.bfloat16)
    _, gelu_back = jax.vjp(gelu_tanh, pre_act)
    grad_rows = lax.all_gather(grad_low, "tensor", axis=0, tiled=True)
    grad_act = jnp.einsum("td,fd->tf", grad_rows, proj_local, preferred_element_type=jnp.float32)
    grad_pre = gelu_back(grad_act)[0].astype(jnp.bfloat16)
    fc_bias_grad = lax.dynamic_update_slice_in_dim(
        jnp.zeros((hidden_width,), jnp.float32),
        jnp.sum(grad_pre.astype(jnp.float32), axis=0),
        hidden_start,
        0,
    )
    fc_grad = jnp.einsum("td,tf->df", normed_two_rows, grad_pre, preferred_element_type=jnp.float32)
    proj_grad = jnp.einsum("tf,td->fd", activated, grad_rows, preferred_element_type=jnp.float32)
    dnormed_two = lax.psum_scatter(
        jnp.einsum("tf,df->td", grad_pre, fc_local, preferred_element_type=jnp.float32).astype(
            jnp.bfloat16
        ),
        "tensor",
        scatter_dimension=0,
        tiled=True,
    ).astype(jnp.float32)
    _, norm_two_back = jax.vjp(layer_norm, resid, vector_params[2], vector_params[3])
    dresid_norm, gain_two_grad, shift_two_grad = norm_two_back(dnormed_two)
    dresid = grad_out + dresid_norm
    out_bias_grad = jnp.sum(dresid, axis=0)
    dresid_low = dresid.astype(jnp.bfloat16)
    dresid_rows = lax.all_gather(dresid_low, "tensor", axis=0, tiled=True)
    dcontext = jnp.einsum(
        "td,jd->tj", dresid_rows, out_local, preferred_element_type=jnp.float32
    ).astype(jnp.bfloat16)
    out_grad = jnp.einsum("tj,td->jd", context, dresid_rows, preferred_element_type=jnp.float32)
    grad_query, grad_key, grad_value = lax.map(
        attend_back,
        (
            split_heads(query_all),
            split_heads(key_all),
            split_heads(value_all),
            segment_blocks,
            log_totals,
            split_heads(dcontext),
        ),
    )
    grad_query = grad_query.reshape(group_rows, local_width).astype(jnp.bfloat16)
    grad_key = grad_key.reshape(group_rows, local_width).astype(jnp.bfloat16)
    grad_value = grad_value.reshape(group_rows, local_width).astype(jnp.bfloat16)
    grad_mixed = jnp.concatenate([grad_query, grad_key, grad_value], axis=1)
    qkv_grad = jnp.einsum(
        "td,tj->dj", normed_rows, grad_mixed, preferred_element_type=jnp.float32
    ).reshape(model_width, 3, local_width)
    query_bias_grad = jnp.sum(grad_query.astype(jnp.float32), axis=0)
    value_bias_grad = jnp.sum(grad_value.astype(jnp.float32), axis=0)
    dnormed_one = lax.psum_scatter(
        jnp.einsum("tj,dj->td", grad_mixed, qkv_flat, preferred_element_type=jnp.float32).astype(
            jnp.bfloat16
        ),
        "tensor",
        scatter_dimension=0,
        tiled=True,
    ).astype(jnp.float32)
    _, norm_one_back = jax.vjp(layer_norm, inputs, vector_params[0], vector_params[1])
    dinput_norm, gain_one_grad, shift_one_grad = norm_one_back(dnormed_one)
    input_grad = (dresid + dinput_norm).astype(jnp.bfloat16)
    head_grads = lax.dynamic_update_slice_in_dim(
        jnp.zeros((2, model_width), jnp.float32),
        jnp.stack([query_bias_grad, value_bias_grad]),
        column_start,
        1,
    )
    vector_grad = jnp.concatenate(
        [
            jnp.stack([gain_one_grad, shift_one_grad, gain_two_grad, shift_two_grad]),
            head_grads,
            jnp.stack([out_bias_grad, proj_bias_grad]),
        ],
        axis=0,
    )
    qkv_grad, out_grad, fc_grad, proj_grad = (
        sum_at_owner(qkv_grad.astype(jnp.bfloat16), "dp", 0),
        sum_at_owner(out_grad.astype(jnp.bfloat16), "dp", 1),
        sum_at_owner(fc_grad.astype(jnp.bfloat16), "dp", 0),
        sum_at_owner(proj_grad.astype(jnp.bfloat16), "dp", 1),
    )
    vector_grad, fc_bias_grad = lax.psum((vector_grad, fc_bias_grad), ("dp", "tensor"))
    local_squares = (
        jnp.sum(qkv_grad * qkv_grad)
        + jnp.sum(out_grad * out_grad)
        + jnp.sum(fc_grad * fc_grad)
        + jnp.sum(proj_grad * proj_grad)
    )
    matrix_squares = lax.psum(local_squares, ("dp", "tensor"))
    grad_norm = jnp.sqrt(
        matrix_squares + jnp.sum(vector_grad * vector_grad) + jnp.sum(fc_bias_grad * fc_bias_grad)
    )
    factor = CLIP_NORM / jnp.maximum(grad_norm, CLIP_NORM)
    qkv_new = adamw_update(
        qkv_weight, qkv_moment1, qkv_moment2, factor * qkv_grad, RATE_MATRIX, WEIGHT_DECAY
    )
    out_new = adamw_update(
        out_weight, out_moment1, out_moment2, factor * out_grad, RATE_MATRIX, WEIGHT_DECAY
    )
    fc_new = adamw_update(
        fc_weight, fc_moment1, fc_moment2, factor * fc_grad, RATE_MATRIX, WEIGHT_DECAY
    )
    proj_new = adamw_update(
        proj_weight, proj_moment1, proj_moment2, factor * proj_grad, RATE_MATRIX, WEIGHT_DECAY
    )
    vector_new = adamw_update(
        vector_params, vector_moment1, vector_moment2, factor * vector_grad, RATE_VECTOR, 0.0
    )
    fc_bias_new = adamw_update(
        fc_bias, fc_bias_moment1, fc_bias_moment2, factor * fc_bias_grad, RATE_VECTOR, 0.0
    )
    return (
        mixed,
        input_grad,
        grad_norm,
        qkv_new[0],
        qkv_new[1],
        qkv_new[2],
        out_new[0],
        out_new[1],
        out_new[2],
        fc_new[0],
        fc_new[1],
        fc_new[2],
        proj_new[0],
        proj_new[1],
        proj_new[2],
        vector_new[0],
        vector_new[1],
        vector_new[2],
        fc_bias_new[0],
        fc_bias_new[1],
        fc_bias_new[2],
    )


def solution(mesh):
    return jax.shard_map(
        on_device,
        mesh=mesh,
        in_specs=(
            P(("dp", "tensor"), None),
            P(("dp", "tensor"), None),
            P("dp"),
            P(("dp", "tensor")),
            P("dp", None, "tensor"),
            P("dp", None, "tensor"),
            P("dp", None, "tensor"),
            P("tensor", "dp"),
            P("tensor", "dp"),
            P("tensor", "dp"),
            P("dp", "tensor"),
            P("dp", "tensor"),
            P("dp", "tensor"),
            P("tensor", "dp"),
            P("tensor", "dp"),
            P("tensor", "dp"),
            P(),
            P(),
            P(),
            P(),
            P(),
            P(),
        ),
        out_specs=(
            P(("dp", "tensor"), None),
            P(("dp", "tensor"), None),
            P(),
            P("dp", None, "tensor"),
            P("dp", None, "tensor"),
            P("dp", None, "tensor"),
            P("tensor", "dp"),
            P("tensor", "dp"),
            P("tensor", "dp"),
            P("dp", "tensor"),
            P("dp", "tensor"),
            P("dp", "tensor"),
            P("tensor", "dp"),
            P("tensor", "dp"),
            P("tensor", "dp"),
            P(),
            P(),
            P(),
            P(),
            P(),
            P(),
        ),
        check_vma=False,
    )
```

profile of v0, /device:TPU:0, one launch (start us, length us, event | category | flops | bytes accessed | tf_op | source)
XLA Modules:
  0.0 805.9 jit_solution(5800812832703071595)
XLA Ops:
  15.3 38.9 %all_gather.25 = bf16[768,3,192]{2,1,0:T(4,128)(2,1)S(1)} all-gather(bf16[96,3,192]{2,1,0:T(4,128)(2,1)S(1)} %copy.102), channel_id=1, replica_groups=mesh['dp'=8,'tensor'=4] {'dp'}, dimensions={0}, use_global_device_ids=true | all-gather | bytes 995328 | tf_op jit(solution)/shard_map/all_gather | solution.py:107
  55.1 31.1 %all_gather.26 = bf16[192,768]{0,1:T(8,128)(2,1)S(1)} all-gather(bf16[192,96]{0,1:T(8,128)(2,1)S(1)} %copy.108), channel_id=1, replica_groups=mesh['dp'=8,'tensor'=4] {'dp'}, dimensions={1}, use_global_device_ids=true | all-gather | bytes 331776 | tf_op jit(solution)/shard_map/all_gather | solution.py:108
  86.3 5.0 fusion.109
  91.4 2.0 fusion.84
  93.4 3.3 reshape.407
  105.8 48.6 %while.30 = (s32[]{:T(128)}, bf16[3,1024,3,64]{1,3,2,0:T(8,128)(2,1)}, f32[3,3,1024,1]{2,1,3,0:T(4,128)}, bf16[3,1024,3,64]{1,3,2,0:T(8,128)(2,1)}, s32[3,1024]{...) while((s32[]{:T(128)}, ...), condition=%wide.region_5.6_spmd, body=%wide.region_2.5_spmd.sunk | while | flops 848303104 | bytes 48228480 | solution.py:167
  107.4 4.2 fusion.155
  111.7 3.9 fusion.156
  115.5 5.7 fusion.157
  123.4 4.2 fusion.155
  127.7 3.9 fusion.156
  131.6 5.7 fusion.157
  139.5 4.2 fusion.155
  143.7 3.9 fusion.156
  147.6 5.7 fusion.157
  154.4 2.3 copy.107
  158.3 3.6 convolution_convert_fusion.3
  163.6 45.3 %reduce-scatter.5.cloned.1.call-done = bf16[768,768]{1,0:T(8,128)(2,1)} async-done(((bf16[3072,768]{1,0:T(8,128)(2,1)}), bf16[768,768]{1,0:T(8,128)(2,1)}) %reduce-scatter.5.cloned.1.call-update) | async-done | bytes 1179664 | tf_op jit(solution)/shard_map/reduce_scatter | solution.py:172
  219.0 32.2 %all-gather.9.cloned.1.call-done = bf16[3072,768]{1,0:T(8,128)(2,1)} async-done(((bf16[768,768]{1,0:T(8,128)(2,1)}), bf16[3072,768]{1,0:T(8,128)(2,1)}) %all-gather.9.cloned.1.call-update) | async-done | bytes 4718608 | tf_op jit(solution)/shard_map/all_gather | solution.py:180
  251.2 10.1 %fusion.110 = f32[3072,768]{1,0:T(8,128)} fusion(bf16[3072,768]{1,0:T(8,128)(2,1)} %all-gather.9.cloned.1.call-done, bf16[768,768]{1,0:T(8,128)(2,1)} %all-gather.11.cloned.1.call-done), kind=kOutput, calls=%fused_computation.204 | convolution fusion | flops 3623878656 | bytes 15335424 | tf_op jit(solution)/shard_map/dot_general | solution.py:181
  261.3 34.3 %all-gather.13.cloned.1.call-done = bf16[768,768]{0,1:T(8,128)(2,1)} async-done(((bf16[768,96]{0,1:T(8,128)(2,1)}), bf16[768,768]{0,1:T(8,128)(2,1)}) %all-gather.13.cloned.1.call-update) | async-done | bytes 1179664 | tf_op jit(solution)/shard_map/all_gather | solution.py:110
  295.6 38.0 %all-gather.15.cloned.1.call-done = bf16[3072,768]{1,0:T(8,128)(2,1)} async-done(((bf16[768,768]{1,0:T(8,128)(2,1)}), bf16[3072,768]{1,0:T(8,128)(2,1)}) %all-gather.15.cloned.1.call-update) | async-done | bytes 4718608 | tf_op jit(solution)/shard_map/all_gather | solution.py:195
  333.7 14.0 %convert_reduce_fusion = (f32[768]{0:T(1024)}, bf16[3072,768]{1,0:T(8,128)(2,1)S(1)}) fusion(f32[3072,768]{1,0:T(8,128)} %fusion.110, f32[768]{0:T(1024)S(1)} %dynamic_slice.74, bf16[3072,768]{1,0:T(8,128)(2,1)} %all-gather.15.cloned.1.call-done, bf16[768,768]{0,1:T(8,128)(2,1)} %all-gather.13.cloned.1.call-done), kind=kOutput, calls=%fused_computation.87 | convolution fusion | flops 3678141696 | bytes 20060160 | tf_op jit(solution)/shard_map/td,fd->tf/dot_general | solution.py:196
  347.7 2.1 copy-done.79
  349.8 5.5 convolution_convert_fusion
  355.6 12.2 %convolution_convert_fusion.1 = bf16[3072,768]{1,0:T(8,128)(2,1)} fusion(bf16[768,768]{0,1:T(8,128)(2,1)} %all-gather.13.cloned.1.call-done, f32[3072,768]{1,0:T(8,128)} %fusion.110, f32[768]{0:T(1024)S(1)} %dynamic_slice.74), kind=kOutput, calls=%fused_computation.90 | convolution fusion | flops 3649830912 | bytes 15338496 | tf_op jit(solution)/shard_map/dot_general | solution.py:184
  367.8 35.5 %reduce-scatter.9.cloned.1.call-done = bf16[768,768]{1,0:T(8,128)(2,1)} async-done(((bf16[3072,768]{1,0:T(8,128)(2,1)}), bf16[768,768]{1,0:T(8,128)(2,1)}) %reduce-scatter.9.cloned.1.call-update) | async-done | bytes 1179664 | tf_op jit(solution)/shard_map/reduce_scatter | solution.py:206
  403.4 3.0 convert_reduce_fusion.2
  407.6 3.1 fusion.82
  411.4 42.2 %reduce-scatter.7.cloned.1.call-done = bf16[768,768]{1,0:T(8,128)(2,1)} async-done(((bf16[3072,768]{1,0:T(8,128)(2,1)}), bf16[768,768]{1,0:T(8,128)(2,1)}) %reduce-scatter.7.cloned.1.call-update) | async-done | bytes 1179664 | tf_op jit(solution)/shard_map/reduce_scatter | solution.py:183
  453.6 4.5 fusion.107
  460.9 37.2 %all-gather.17.cloned.1.call-done = bf16[3072,768]{1,0:T(8,128)(2,1)} async-done(((bf16[768,768]{1,0:T(8,128)(2,1)}), bf16[3072,768]{1,0:T(8,128)(2,1)}) %all-gather.17.cloned.1.call-update) | async-done | bytes 4718608 | tf_op jit(solution)/shard_map/all_gather | solution.py:219
  498.1 4.0 convolution_convert_fusion.4
  507.9 82.7 %while.31 = (s32[]{:T(128)}, bf16[3,1024,3,64]{1,3,2,0:T(8,128)(2,1)}, bf16[3,1024,3,64]{1,3,2,0:T(8,128)(2,1)}, bf16[3,1024,3,64]{1,3,2,0:T(8,128)(2,1)S(1)}, b...) while((s32[]{:T(128)}, ...), condition=%wide.region_15.16_spmd, body=%wide.region_13.15_spmd.sunk | while | flops 2066093056 | bytes 127390984 | solution.py:224
  512.0 3.7 fusion.170
  515.7 8.1 %multiply_reduce_fusion.9 = (f32[3,1024]{1,0:T(4,128)S(1)}, f32[3,1024,1024]{1,2,0:T(8,128)}) fusion(f32[3,1024,1024]{1,2,0:T(8,128)S(1)} %fusion.166, f32[3,1024]{1,0:T(4,128)S(1)} %dynamic-slice_bitcast_fusion.2, pred[1024,1024]{0,1:T(8,128)(4,1)S(1)} %fusion.167, bf16[3,1024,3,64]{1,3,2,0:T(8,128)(2,1)} %get-tuple-element.613, s32[]{:T(128)S(6)} %copy.155, ...), kind=kOutput, calls=%fused_computation.31.clone.1 | convolution fusion | flops 418378752 | bytes 27030528 | tf_op jit(solution)/shard_map/while/body/eval_jaxpr/qhe,khe->hqk/dot_general | solution.py:138
  523.9 7.0 multiply_convert_fusion.5
  531.0 2.0 fusion.169
  539.4 3.7 fusion.170
  543.2 8.1 %multiply_reduce_fusion.9 = (f32[3,1024]{1,0:T(4,128)S(1)}, f32[3,1024,1024]{1,2,0:T(8,128)}) fusion(f32[3,1024,1024]{1,2,0:T(8,128)S(1)} %fusion.166, f32[3,1024]{1,0:T(4,128)S(1)} %dynamic-slice_bitcast_fusion.2, pred[1024,1024]{0,1:T(8,128)(4,1)S(1)} %fusion.167, bf16[3,1024,3,64]{1,3,2,0:T(8,128)(2,1)} %get-tuple-element.613, s32[]{:T(128)S(6)} %copy.155, ...), kind=kOutput, calls=%fused_computation.31.clone.1 | convolution fusion | flops 418378752 | bytes 27030528 | tf_op jit(solution)/shard_map/while/body/eval_jaxpr/qhe,khe->hqk/dot_general | solution.py:138
  551.3 7.0 multiply_convert_fusion.5
  558.4 2.0 fusion.169
  566.9 3.7 fusion.170
  570.6 8.1 %multiply_reduce_fusion.9 = (f32[3,1024]{1,0:T(4,128)S(1)}, f32[3,1024,1024]{1,2,0:T(8,128)}) fusion(f32[3,1024,1024]{1,2,0:T(8,128)S(1)} %fusion.166, f32[3,1024]{1,0:T(4,128)S(1)} %dynamic-slice_bitcast_fusion.2, pred[1024,1024]{0,1:T(8,128)(4,1)S(1)} %fusion.167, bf16[3,1024,3,64]{1,3,2,0:T(8,128)(2,1)} %get-tuple-element.613, s32[]{:T(128)S(6)} %copy.155, ...), kind=kOutput, calls=%fused_computation.31.clone.1 | convolution fusion | flops 418378752 | bytes 27030528 | tf_op jit(solution)/shard_map/while/body/eval_jaxpr/qhe,khe->hqk/dot_general | solution.py:138
  578.7 7.0 multiply_convert_fusion.5
  585.8 2.0 fusion.169
  590.5 2.3 copy.113
  598.6 5.6 convolution_convert_fusion.2
  604.3 8.7 %convolution_convert_fusion.6 = bf16[768,768]{1,0:T(8,128)(2,1)} fusion(bf16[3072,768]{1,0:T(8,128)(2,1)} %all-gather.9.cloned.1.call-done, bf16[3072,768]{1,0:T(8,128)(2,1)} %copy-done.79), kind=kOutput, calls=%fused_computation.142 | convolution fusion | flops 3624468480 | bytes 10616832 | tf_op jit(solution)/shard_map/td,tf->df/dot_general | solution.py:204
  613.0 5.8 all-to-all-start.2
  618.9 11.3 %convolution_convert_fusion.5 = bf16[768,768]{0,1:T(8,128)(2,1)} fusion(bf16[3072,768]{1,0:T(8,128)(2,1)} %all-gather.15.cloned.1.call-done, f32[3072,768]{1,0:T(8,128)} %fusion.110, f32[768]{0:T(1024)S(1)} %copy-done.77), kind=kOutput, calls=%fused_computation.141 | convolution fusion | flops 3648061440 | bytes 15338496 | tf_op jit(solution)/shard_map/tf,td->fd/dot_general | solution.py:205
  630.2 17.6 %all-to-all-done.2 = bf16[8,96,768]{2,1,0:T(8,128)(2,1)S(1)} async-done(((bf16[8,96,768]{2,1,0:T(8,128)(2,1)}), bf16[8,96,768]{2,1,0:T(8,128)(2,1)S(1)}, u32[]{:S(2)}, u32[]{:S(2)}) %all-to-all-start.2) | async-done | bytes 1179680 | tf_op jit(solution)/shard_map/all_to_all | solution.py:31
  647.8 4.3 all-to-all-start.3
  652.1 4.1 convolution_convert_fusion.8
  658.4 22.0 %all-to-all-done.3 = bf16[8,768,96]{1,2,0:T(8,128)(2,1)} async-done(((bf16[8,768,96]{1,2,0:T(8,128)(2,1)}), bf16[8,768,96]{1,2,0:T(8,128)(2,1)}, u32[]{:S(2)}, u32[]{:S(2)}) %all-to-all-start.3) | async-done | bytes 1179680 | tf_op jit(solution)/shard_map/all_to_all | solution.py:31
  680.4 3.5 all-to-all-start.1
  683.9 7.2 convolution_convert_fusion.7
  691.1 2.4 convert_element_type.197
  695.8 5.5 all-to-all-start
  715.6 14.0 %all-to-all-done = bf16[8,96,3,192]{1,3,2,0:T(8,128)(2,1)} async-done(((bf16[8,96,3,192]{1,3,2,0:T(8,128)(2,1)}), bf16[8,96,3,192]{1,3,2,0:T(8,128)(2,1)}, u32[]{:S(2)}, u32[]{:S(2)}) %all-to-all-start) | async-done | bytes 884768 | tf_op jit(solution)/shard_map/all_to_all | solution.py:31
  734.5 2.2 convert_reduce_fusion.1
  738.8 37.7 %all-reduce = (f32[]{:T(128)}, f32[8,768]{1,0:T(8,128)S(1)}, f32[3072]{0:T(1024)S(1)}) all-reduce(f32[]{:T(128)S(6)} %add.331, f32[8,768]{1,0:T(8,128)S(1)} %concatenate.7, f32[3072]{0:T(1024)} %dynamic_update_slice.39), channel_id=1, replica_groups=mesh['dp'=8,'tensor'=4] {'dp','tensor'}, use_global_device_ids=true, to_apply=%region_27.28 | all-reduce | flops 9217 | bytes 73736 | tf_op jit(solution)/shard_map/psum | solution.py:282
  779.8 2.2 multiply_subtract_fusion.2
  792.3 2.1 multiply_subtract_fusion
  (327 shorter events, 110.2 us)
Async XLA Ops:
  8.0 5.4 copy-start
  8.0 4.1 copy-start.53
  8.0 78.2 %all-gather.7.cloned.1.call-start = ((), (), s32[]{:S(2)}) async-start(), calls=%async_computation.8 | async-start | bytes 5898240 | tf_op jit(solution)/shard_map/all_gather | solution.py:161
  9.7 5.3 copy-start.70
  9.7 5.3 copy-start.40
  9.7 5.4 copy-start.35
  14.9 194.0 %reduce-scatter.5.cloned.1.call-start = ((), (), s32[]{:S(2)}) async-start(), calls=%async_computation.9 | async-start | bytes 5898240 | tf_op jit(solution)/shard_map/reduce_scatter | solution.py:172
  55.0 31.2 %copy-start.37 = (bf16[768,3,192]{0,2,1:T(8,128)(2,1)}, bf16[768,3,192]{0,2,1:T(8,128)(2,1)S(1)}, u32[]{:S(2)}) copy-start(bf16[768,3,192]{0,2,1:T(8,128)(2,1)S(1)} %copy.103) | copy-start | bytes 2654212
  86.3 71.0 %copy-start.24 = (bf16[192,768]{0,1:T(8,128)(2,1)}, bf16[192,768]{0,1:T(8,128)(2,1)S(1)}, u32[]{:S(2)}) copy-start(bf16[192,768]{0,1:T(8,128)(2,1)S(1)} %all_gather.26) | copy-start | bytes 884740
  107.4 4.3 copy-start.3
  123.4 4.3 copy-start.3
  139.5 4.3 copy-start.3
  161.9 47.1 %copy-start.1 = (bf16[768,768]{1,0:T(8,128)(2,1)S(1)}, bf16[768,768]{1,0:T(8,128)(2,1)}, u32[]{:S(2)}) copy-start(bf16[768,768]{1,0:T(8,128)(2,1)} %param.26) | copy-start | bytes 3538948
  161.9 47.1 %copy-start.45 = (f32[768]{0:T(1024)S(1)}, f32[768]{0:T(1024)}, u32[]{:S(2)}) copy-start(f32[768]{0:T(1024)} %get-tuple-element.440) | copy-start | bytes 9220
  161.9 57.1 %all-gather.11.cloned.1.call-start = ((), (), s32[]{:S(2)}) async-start(), calls=%async_computation.11 | async-start | bytes 1327104 | tf_op jit(solution)/shard_map/all_gather | solution.py:109
  163.5 87.7 %all-gather.9.cloned.1.call-start = ((), (), s32[]{:S(2)}) async-start(), calls=%async_computation.10 | async-start | bytes 5898240 | tf_op jit(solution)/shard_map/all_gather | solution.py:180
  212.1 4.8 copy-start.19
  213.8 81.8 %all-gather.13.cloned.1.call-start = ((), (), s32[]{:S(2)}) async-start(), calls=%async_computation.12 | async-start | bytes 1327104 | tf_op jit(solution)/shard_map/all_gather | solution.py:110
  215.5 118.2 %all-gather.15.cloned.1.call-start = ((), (), s32[]{:S(2)}) async-start(), calls=%async_computation.14 | async-start | bytes 5898240 | tf_op jit(solution)/shard_map/all_gather | solution.py:195
  218.2 185.2 %reduce-scatter.9.cloned.1.call-start = ((), (), s32[]{:S(2)}) async-start(), calls=%async_computation.15 | async-start | bytes 5898240 | tf_op jit(solution)/shard_map/reduce_scatter | solution.py:206
  219.0 136.6 %copy-start.76 = (f32[768]{0:T(1024)}, f32[768]{0:T(1024)S(1)}, u32[]{:S(2)}) copy-start(f32[768]{0:T(1024)S(1)} %dynamic_slice.74) | copy-start | bytes 9220
  333.7 16.1 %copy-start.78 = (bf16[768,768]{1,0:T(8,128)(2,1)S(1)}, bf16[768,768]{1,0:T(8,128)(2,1)}, u32[]{:S(2)}) copy-start(bf16[768,768]{1,0:T(8,128)(2,1)} %all-gather.11.cloned.1.call-done) | copy-start | bytes 3538948
  355.4 98.2 %reduce-scatter.7.cloned.1.call-start = ((), (), s32[]{:S(2)}) async-start(), calls=%async_computation.13 | async-start | bytes 5898240 | tf_op jit(solution)/shard_map/reduce_scatter | solution.py:183
  367.8 130.3 %all-gather.17.cloned.1.call-start = ((), (), s32[]{:S(2)}) async-start(), calls=%async_computation.16 | async-start | bytes 5898240 | tf_op jit(solution)/shard_map/all_gather | solution.py:219
  403.4 4.3 copy-start.13
  459.5 38.6 %copy-start.25 = (bf16[192,768]{0,1:T(8,128)(2,1)S(1)}, bf16[192,768]{0,1:T(8,128)(2,1)}, u32[]{:S(2)}) copy-start(bf16[192,768]{0,1:T(8,128)(2,1)} %copy-done.24) | copy-start | bytes 884740
  460.7 273.8 %reduce-scatter.11.cloned.1.call-start = ((), (), s32[]{:S(2)}) async-start(), calls=%async_computation.17 | async-start | bytes 5898240 | tf_op jit(solution)/shard_map/reduce_scatter | solution.py:244
  523.9 7.0 copy-start.20
  551.3 7.0 copy-start.20
  578.7 7.0 copy-start.20
  613.0 5.9 copy-start.77
  613.0 34.8 %all-to-all-start.2 = ((bf16[8,96,768]{2,1,0:T(8,128)(2,1)}), bf16[8,96,768]{2,1,0:T(8,128)(2,1)S(1)}, u32[]{:S(2)}, u32[]{:S(2)}) async-start(bf16[8,96,768]{2,1,0:T(8,128)(2,1)} %bitcast.23), calls=%async_computation.6 | async-start | bytes 2359296 | tf_op jit(solution)/shard_map/all_to_all | solution.py:31
  630.2 21.9 %copy-start.16 = (bf16[24,8,3,1024]{3,1,2,0:T(8,128)(2,1)S(1)}, bf16[24,8,3,1024]{3,1,2,0:T(8,128)(2,1)}, u32[]{:S(2)}) copy-start(bf16[24,8,3,1024]{3,1,2,0:T(8,128)(2,1)} %copy-done.15) | copy-start | bytes 3538948
  647.8 8.4 %copy-start.17 = (bf16[8,96,768]{2,1,0:T(8,128)(2,1)}, bf16[8,96,768]{2,1,0:T(8,128)(2,1)S(1)}, u32[]{:S(2)}) copy-start(bf16[8,96,768]{2,1,0:T(8,128)(2,1)S(1)} %all-to-all-done.2) | copy-start | bytes 3538948
  647.8 32.6 %all-to-all-start.3 = ((bf16[8,768,96]{1,2,0:T(8,128)(2,1)}), bf16[8,768,96]{1,2,0:T(8,128)(2,1)}, u32[]{:S(2)}, u32[]{:S(2)}) async-start(bf16[8,768,96]{1,2,0:T(8,128)(2,1)} %bitcast.178), calls=%async_computation.7 | async-start | bytes 2359296 | tf_op jit(solution)/shard_map/all_to_all | solution.py:31
  680.4 15.3 %all-to-all-start.1 = ((bf16[8,192,96]{2,1,0:T(8,128)(2,1)}), bf16[8,192,96]{2,1,0:T(8,128)(2,1)S(1)}, u32[]{:S(2)}, u32[]{:S(2)}) async-start(bf16[8,192,96]{2,1,0:T(8,128)(2,1)} %bitcast.128), calls=%async_computation.5 | async-start | bytes 786432 | tf_op jit(solution)/shard_map/all_to_all | solution.py:31
  693.5 7.8 copy-start.36
  693.5 8.6 %copy-start.44 = (f32[96,3,192]{2,0,1:T(8,128)S(1)}, f32[96,3,192]{2,0,1:T(8,128)}, u32[]{:S(2)}) copy-start(f32[96,3,192]{2,0,1:T(8,128)} %param.31) | copy-start | bytes 663556
  694.8 10.6 %copy-start.75 = (f32[768]{0:T(1024)S(1)}, f32[768]{0:T(1024)}, u32[]{:S(2)}) copy-start(f32[768]{0:T(1024)} %get-tuple-element.424) | copy-start | bytes 9220
  694.8 12.1 %copy-start.18 = (bf16[8,96,768]{2,1,0:T(8,128)(2,1)S(1)}, bf16[8,96,768]{2,1,0:T(8,128)(2,1)}, u32[]{:S(2)}) copy-start(bf16[8,96,768]{2,1,0:T(8,128)(2,1)} %copy-done.17) | copy-start | bytes 3538948
  695.7 9.7 %copy-start.30 = (bf16[8,192,96]{2,1,0:T(8,128)(2,1)}, bf16[8,192,96]{2,1,0:T(8,128)(2,1)S(1)}, u32[]{:S(2)}) copy-start(bf16[8,192,96]{2,1,0:T(8,128)(2,1)S(1)} %all-to-all-done.1) | copy-start | bytes 884740
  695.8 33.8 %all-to-all-start = ((bf16[8,96,3,192]{1,3,2,0:T(8,128)(2,1)}), bf16[8,96,3,192]{1,3,2,0:T(8,128)(2,1)}, u32[]{:S(2)}, u32[]{:S(2)}) async-start(bf16[8,96,3,192]{1,3,2,0:T(8,128)(2,1)} %copy.116), calls=%async_computation.4 | async-start | bytes 2359296 | tf_op jit(solution)/shard_map/all_to_all | solution.py:31
  702.1 7.9 copy-start.68
  702.1 8.4 %copy-start.69 = (f32[768]{0:T(1024)S(1)}, f32[768]{0:T(1024)}, u32[]{:S(2)}) copy-start(f32[768]{0:T(1024)} %get-tuple-element.355) | copy-start | bytes 9220
  702.1 9.0 %copy-start.65 = (f32[768]{0:T(1024)S(1)}, f32[768]{0:T(1024)}, u32[]{:S(2)}) copy-start(f32[768]{0:T(1024)} %get-tuple-element.426) | copy-start | bytes 9220
  702.1 9.6 %copy-start.64 = (f32[768]{0:T(1024)S(1)}, f32[768]{0:T(1024)}, u32[]{:S(2)}) copy-start(f32[768]{0:T(1024)} %get-tuple-element.435) | copy-start | bytes 9220
  706.9 5.8 copy-start.12
  707.0 4.7 copy-start.26
  712.3 22.2 %copy-start.2 = (bf16[768,768]{1,0:T(8,128)(2,1)S(1)}, bf16[768,768]{1,0:T(8,128)(2,1)}, u32[]{:S(2)}) copy-start(bf16[768,768]{1,0:T(8,128)(2,1)} %param.26) | copy-start | bytes 3538948
  712.3 22.2 %copy-start.48 = (f32[768]{0:T(1024)S(1)}, f32[768]{0:T(1024)}, u32[]{:S(2)}) copy-start(f32[768]{0:T(1024)} %copy-done.47) | copy-start | bytes 9220
  712.3 22.2 %copy-start.51 = (f32[768]{0:T(1024)S(1)}, f32[768]{0:T(1024)}, u32[]{:S(2)}) copy-start(f32[768]{0:T(1024)} %copy-done.50) | copy-start | bytes 9220
  713.2 23.5 %copy-start.61 = (f32[768]{0:T(1024)S(1)}, f32[768]{0:T(1024)}, u32[]{:S(2)}) copy-start(f32[768]{0:T(1024)} %copy-done.60) | copy-start | bytes 9220
  713.2 23.5 %copy-start.56 = (f32[768]{0:T(1024)S(1)}, f32[768]{0:T(1024)}, u32[]{:S(2)}) copy-start(f32[768]{0:T(1024)} %copy-done.55) | copy-start | bytes 9220
  734.4 3.7 copy-start.71
  734.4 3.7 copy-start.72
  734.4 45.3 %copy-start.34 = (f32[96,3,192]{0,2,1:T(8,128)S(1)}, f32[96,3,192]{0,2,1:T(8,128)}, u32[]{:S(2)}) copy-start(f32[96,3,192]{0,2,1:T(8,128)} %copy.122) | copy-start | bytes 663556
  779.7 12.6 %copy-start.29 = (f32[768,96]{0,1:T(8,128)S(1)}, f32[768,96]{0,1:T(8,128)}, u32[]{:S(2)}) copy-start(f32[768,96]{0,1:T(8,128)} %copy-done.28) | copy-start | bytes 884740
  779.8 12.6 %copy-start.31 = (f32[768,96]{0,1:T(8,128)S(1)}, f32[768,96]{0,1:T(8,128)}, u32[]{:S(2)}) copy-start(f32[768,96]{0,1:T(8,128)} %param.39) | copy-start | bytes 884740
  781.9 12.5 %copy-start.27 = (f32[96,768]{1,0:T(8,128)S(1)}, f32[96,768]{1,0:T(8,128)}, u32[]{:S(2)}) copy-start(f32[96,768]{1,0:T(8,128)} %copy-done.26) | copy-start | bytes 884740
  781.9 12.5 %copy-start.33 = (f32[96,768]{1,0:T(8,128)S(1)}, f32[96,768]{1,0:T(8,128)}, u32[]{:S(2)}) copy-start(f32[96,768]{1,0:T(8,128)} %param.36) | copy-start | bytes 884740
  787.5 6.9 copy-start.42
  787.5 6.9 copy-start.43
  790.4 5.1 copy-start.8
  790.4 5.1 copy-start.66
  (42 other events, 75.6 us)
Sparse Core Ops, SparseCore 0:
  15.1 40.1 all-gather.6
  162.0 46.8 reduce-scatter.4
  355.5 47.8 reduce-scatter.8
  405.7 47.8 reduce-scatter.6
Sparse Core Ops, SparseCore 1:
  165.4 40.5 all-gather.10
  213.9 37.3 all-gather.8
  254.1 41.5 all-gather.12
  297.9 35.8 all-gather.14
  460.8 37.3 all-gather.16
  604.4 47.7 reduce-scatter.10
where the time goes:
time: 817 us; the launch traced here: 806 us
  waiting for transfers between devices  320 us (39%)
  matrix products  172 us (21%)
  blocking collectives  108 us (13%)
  other arithmetic  97.2 us (12%)
  local copies, waits for them, and re-layouts  66.1 us (8%)
  between operations  22.2 us (3%)
  starting transfers between devices  19.9 us (2%)
    all_to_all x4, waiting for transfers between devices, sum_at_owner(): lax.all_to_all(cut_along(shard, dim, devices), axis, 0, 0, tiled=True)  54.5 us
    reduce_scatter x1, waiting for transfers between devices, on_device(): lax.psum_scatter(jnp.dot(context, out_local, preferred_element_type=jnp.f...  45.3 us
    reduce_scatter x1, waiting for transfers between devices, on_device(): lax.psum_scatter(jnp.dot(activated, proj_local, preferred_element_type=jn...  42.2 us
    all_gather x1, blocking collectives, on_device(): lax.all_gather(qkv_weight.astype(jnp.bfloat16), 'dp', axis=0, tiled=True)  38.9 us
    all_gather x1, waiting for transfers between devices, on_device(): grad_rows = lax.all_gather(grad_low, 'tensor', axis=0, tiled=True)  38 us
    psum x1, blocking collectives, on_device(): matrix_squares = lax.psum(local_squares, ('dp', 'tensor'))  37.7 us
    all_gather x1, waiting for transfers between devices, on_device(): dresid_rows = lax.all_gather(dresid_low, 'tensor', axis=0, tiled=True)  37.2 us
    reduce_scatter x1, waiting for transfers between devices, on_device(): lax.psum_scatter(jnp.einsum('tf,df->td', grad_pre, fc_local, preferred_el...  35.5 us
  transfers between devices with their start and end apart: 14, of which 11 were waited for; matrix products, arithmetic and copies ran while one was open for 12% of the time, Pallas kernels for 0%

commit v1 on v0

v1 whole, which is shorter than its diff:
```python
import functools
import math

import jax
import jax.numpy as jnp
from jax import lax
from jax.experimental import pallas as pl
from jax.experimental.pallas import tpu as pltpu
from jax.sharding import PartitionSpec as P

HD = 64
SLOT = 1024
STEP = 10
NORM_EPSILON = 1e-05
MASK_FILL = -1e30
DECAY_FIRST = 0.5
DECAY_SECOND = 0.5
ADAM_EPSILON = 1e-08
WEIGHT_DECAY = 0.1
CLIP_NORM = 1.0
RATE_MATRIX = 0.04
RATE_VECTOR = 0.3

MESH = pl.DeviceIdType.MESH
BF = jnp.bfloat16
F32 = jnp.float32
HALF = SLOT // 2
BLK = 256
VMEM_LIMIT = 58 * 2**20
LOG2E = math.log2(math.e)
SCORE_SCALE = float(HD) ** (-0.5)
SCORE_SCALE2 = SCORE_SCALE * LOG2E


def dot_nn(a, b):
    return lax.dot_general(a, b, (((1,), (0,)), ((), ())), preferred_element_type=F32)


def dot_nt(a, b):
    return lax.dot_general(a, b, (((1,), (1,)), ((), ())), preferred_element_type=F32)


def dot_tn(a, b):
    return lax.dot_general(a, b, (((0,), (0,)), ((), ())), preferred_element_type=F32)


def dot_tt(a, b):
    return lax.dot_general(a, b, (((0,), (1,)), ((), ())), preferred_element_type=F32)


def params(collective_id=None):
    if collective_id is None:
        return pltpu.CompilerParams(vmem_limit_bytes=VMEM_LIMIT)
    return pltpu.CompilerParams(
        vmem_limit_bytes=VMEM_LIMIT, collective_id=collective_id, has_side_effects=True
    )


VM = pl.BlockSpec(memory_space=pltpu.VMEM)
ANY = pl.BlockSpec(memory_space=pl.ANY)


def sds(shape, dtype):
    return jax.ShapeDtypeStruct(shape, dtype)


def here():
    t = lax.axis_index("tensor")
    return lax.axis_index("dp"), t // 2, t % 2


def greet(ids):
    sem = pltpu.get_barrier_semaphore()
    for one in ids:
        pl.semaphore_signal(sem, inc=1, device_id=one, device_id_type=MESH)
    pl.semaphore_wait(sem, len(ids))


def remote(src, dst, send_sem, recv_sem, target):
    return pltpu.make_async_remote_copy(
        src_ref=src,
        dst_ref=dst,
        send_sem=send_sem,
        recv_sem=recv_sem,
        device_id=target,
        device_id_type=MESH,
    )


def rows_at(start, size):
    return pl.ds(pl.multiple_of(start, size), size)


def norm_parts(values):
    centered = values - jnp.mean(values, axis=-1, keepdims=True)
    variance = jnp.mean(centered * centered, axis=-1, keepdims=True)
    scale = lax.rsqrt(variance + NORM_EPSILON)
    return centered * scale, scale


def share_kernel(tok_ref, grad_ref, tk_ref, gl_ref, loc, ss, rs):
    dp, x, c = here()
    core = (dp, x * 2 + 1 - c)
    across = [(dp, (1 - x) * 2), (dp, (1 - x) * 2 + 1)]
    greet([core] + across)
    rows = tok_ref.shape[0]
    tk_rows = rows_at(x * HALF + c * rows, BLK)
    tk_rows = pl.ds(pl.multiple_of(x * HALF + c * rows, BLK), rows)
    gl_rows = pl.ds(pl.multiple_of(c * rows, BLK), rows)
    mine = [
        pltpu.make_async_copy(tok_ref, tk_ref.at[tk_rows], loc.at[0]),
        pltpu.make_async_copy(grad_ref, gl_ref.at[gl_rows], loc.at[1]),
    ]
    out = [
        remote(tok_ref, tk_ref.at[tk_rows], ss.at[0], rs.at[0], core),
        remote(grad_ref, gl_ref.at[gl_rows], ss.at[1], rs.at[1], core),
    ]
    half_src = tok_ref.at[pl.ds(pl.multiple_of((1 - x) * BLK, BLK), HALF)]
    half_dst = tk_ref.at[pl.ds(pl.multiple_of(x * (SLOT + HALF), HALF), HALF)]
    halves = [
        remote(half_src, half_dst, ss.at[2 + k], rs.at[2], across[k]) for k in range(2)
    ]

    @pl.when(c == 1 - x)
    def _():
        for one in halves:
            one.start()

    for one in mine + out:
        one.start()
    for one in mine + out:
        one.wait()
    halves[0].wait_recv()

    @pl.when(c == 1 - x)
    def _():
        for one in halves:
            one.wait_send()


def share_tokens(tokens, grad_low):
    rows, width = tokens.shape
    return pl.pallas_call(
        share_kernel,
        out_shape=(sds((2 * SLOT, width), BF), sds((2 * rows, width), BF)),
        in_specs=[ANY, ANY],
        out_specs=(ANY, ANY),
        scratch_shapes=[
            pltpu.SemaphoreType.DMA((2,)),
            pltpu.SemaphoreType.DMA((4,)),
            pltpu.SemaphoreType.DMA((3,)),
        ],
        compiler_params=params(1),
        name="share_tokens",
    )(tokens, grad_low)


def gather_kernel(n, *refs):
    shards, outs = refs[:n], refs[n : 2 * n]
    loc, ss, rs = refs[2 * n :]
    dp, x, c = here()
    z, y = dp // 2, dp % 2
    me = x * 2 + c
    z_peers = [(lax.rem(z + k, 4) * 2 + y, me) for k in (1, 2, 3)]
    x_peer = (dp, (1 - x) * 2 + c)
    y_peer = (z * 2 + 1 - y, me)
    greet(z_peers + [x_peer, y_peer])
    owns, zs, xys, fs = [], [], [], []
    for a in range(n):
        block = outs[a].at[x, z, y]
        owns.append(pltpu.make_async_copy(shards[a], block, loc.at[a]))
        zs.append(
            [remote(shards[a], block, ss.at[a, k], rs.at[a, k], z_peers[k]) for k in range(3)]
        )
        column = outs[a].at[x, :, y]
        xys.append(
            [
                remote(column, column, ss.at[a, 3], rs.at[a, 3], x_peer),
                remote(column, column, ss.at[a, 4], rs.at[a, 4], y_peer),
            ]
        )
        from_x = outs[a].at[1 - x, pl.ds(0, 2), y]
        from_y = outs[a].at[x, pl.ds(2, 2), 1 - y]
        fs.append(
            [
                remote(from_x, from_x, ss.at[a, 5], rs.at[a, 5], y_peer),
                remote(from_y, from_y, ss.at[a, 6], rs.at[a, 6], x_peer),
            ]
        )
    for a in range(n):
        owns[a].start()
        for one in zs[a]:
            one.start()
    for a in range(n + 1):
        if a < n:
            owns[a].wait()
            for one in zs[a]:
                one.wait()
            for one in xys[a]:
                one.start()
        if a > 0:
            for one in xys[a - 1]:
                one.wait()
            for one in fs[a - 1]:
                one.start()
    for a in range(n):
        for one in fs[a]:
            one.wait()


def gather_weights(shards):
    n = len(shards)
    if lax.axis_size("dp") != 8:
        slot = lax.axis_index("tensor") // 2
        swap = [(0, 2), (1, 3), (2, 0), (3, 1)]
        result = []
        for shard in shards:
            own = lax.all_gather(shard, "dp", axis=0, tiled=True)
            other = lax.ppermute(own, "tensor", swap)
            result.append(
                jnp.stack([jnp.where(slot == 0, own, other), jnp.where(slot == 0, other, own)])
            )
        return result
    shapes = [(2, 4, 2) + s.shape for s in shards]
    outs = pl.pallas_call(
        functools.partial(gather_kernel, n),
        out_shape=tuple(sds(s, BF) for s in shapes),
        in_specs=[ANY] * n,
        out_specs=(ANY,) * n,
        scratch_shapes=[
            pltpu.SemaphoreType.DMA((n,)),
            pltpu.SemaphoreType.DMA((n, 7)),
            pltpu.SemaphoreType.DMA((n, 7)),
        ],
        compiler_params=params(2),
        name="gather_weights",
    )(*shards)
    return [o.reshape(2, 8 * s.shape[0], s.shape[1]) for o, s in zip(outs, shards, strict=True)]


def qkv_kernel(tk_ref, vec_ref, bias_ref, wq_ref, n1_ref, u_ref):
    _, x, _ = here()
    gain, shift = vec_ref[0:1, :], vec_ref[1:2, :]

    def norm(i, carry):
        rows = rows_at(i * BLK, BLK)
        unit, _ = norm_parts(tk_ref[rows, :].astype(F32))
        n1_ref[rows, :] = (unit * gain + shift).astype(BF)
        return carry

    lax.fori_loop(0, 2 * SLOT // BLK, norm, 0)

    def project(i, carry):
        lanes = rows_at(i * BLK, BLK)
        full = n1_ref[rows_at(x * SLOT + i * BLK, BLK), :]
        u_ref[0, :, lanes] = (dot_tt(wq_ref[0], full) + bias_ref[0]).astype(BF)
        u_ref[1, :, lanes] = (dot_tt(wq_ref[1], full) + bias_ref[1]).astype(BF)
        part = n1_ref[rows_at((1 - x) * SLOT + i * BLK, BLK), :]
        u_ref[2, :, lanes] = (dot_tt(wq_ref[x], part) + bias_ref[x]).astype(BF)
        return carry

    lax.fori_loop(0, SLOT // BLK, project, 0)


def project_qkv(tk, vectors, bias, wq):
    cols = wq.shape[2]
    return pl.pallas_call(
        qkv_kernel,
        out_shape=(sds(tk.shape, BF), sds((3, cols, SLOT), BF)),
        in_specs=[VM] * 4,
        out_specs=(VM, VM),
        compiler_params=params(),
        name="norm_qkv",
    )(tk, vectors, bias, wq)


def allowed_pairs(key_block, query_block, start_row, wide):
    keys = lax.broadcasted_iota(jnp.int32, (BLK, wide), 0) + key_block * BLK
    mask = keys >= start_row
    if key_block == query_block:
        queries = lax.broadcasted_iota(jnp.int32, (BLK, wide), 1) + query_block * BLK
        mask = mask & (keys <= queries)
    return mask


def attend_unit(q, k, v, start):
    blocks = SLOT // BLK
    for i in range(blocks):
        cols = slice(i * BLK, (i + 1) * BLK)
        query = q(cols)
        scores = []
        for j in range(i + 1):
            raw = dot_tn(k(slice(j * BLK, (j + 1) * BLK)), query) * SCORE_SCALE2
            scores.append(jnp.where(allowed_pairs(j, i, start(cols), BLK), raw, MASK_FILL))
        top = functools.reduce(jnp.maximum, [jnp.max(s, axis=0, keepdims=True) for s in scores])
        exps = [jnp.exp2(s - top) for s in scores]
        total = functools.reduce(jnp.add, [jnp.sum(e, axis=0, keepdims=True) for e in exps])
        acc = None
        for j in range(i + 1):
            term = dot_nn(v(slice(j * BLK, (j + 1) * BLK)), exps[j].astype(BF))
            acc = term if acc is None else acc + term
        yield cols, acc / total, top + jnp.log2(total)


def attend_kernel(u_ref, start_ref, ctx_ref, lse_ref):
    for cols, context, log_total in attend_unit(
        lambda s: u_ref[0, 0, 0, :, s],
        lambda s: u_ref[0, 1, 0, :, s],
        lambda s: u_ref[0, 2, 0, :, s],
        lambda s: start_ref[0, :, s],
    ):
        ctx_ref[0, 0, :, cols] = context.astype(BF)
        lse_ref[0, 0, :, cols] = log_total


def attend(units, starts):
    groups, _, heads = units.shape[:3]
    return pl.pallas_call(
        attend_kernel,
        grid=(groups, heads),
        out_shape=(sds((groups, heads, HD, SLOT), BF), sds((groups, heads, 1, SLOT), F32)),
        in_specs=[
            pl.BlockSpec((1, 3, 1, HD, SLOT), lambda g, h: (g, 0, h, 0, 0)),
            pl.BlockSpec((1, 1, SLOT), lambda g, h: (g // 2, 0, 0)),
        ],
        out_specs=(
            pl.BlockSpec((1, 1, HD, SLOT), lambda g, h: (g, h, 0, 0)),
            pl.BlockSpec((1, 1, 1, SLOT), lambda g, h: (g, h, 0, 0)),
        ),
        compiler_params=params(),
        name="attend",
    )(units, starts)


def attend_back_kernel(u_ref, start_ref, ctx_ref, dctx_ref, lse_ref, out_ref, dq_ref):
    blocks = SLOT // BLK
    dctx = dctx_ref[0, 0]
    delta = jnp.sum(dctx.astype(F32) * ctx_ref[0, 0].astype(F32), axis=0, keepdims=True)
    start = start_ref[0]
    lse = lse_ref[0, 0]
    for j in range(blocks):
        keys = slice(j * BLK, (j + 1) * BLK)
        k = u_ref[0, 1, 0, :, keys]
        v = u_ref[0, 2, 0, :, keys]
        probs, dscores = [], []
        for i in range(j, blocks):
            cols = slice(i * BLK, (i + 1) * BLK)
            raw = dot_tn(k, u_ref[0, 0, 0, :, cols]) * SCORE_SCALE2 - lse[:, cols]
            prob = jnp.exp2(jnp.where(allowed_pairs(j, i, start[:, cols], BLK), raw, MASK_FILL))
            dprob = dot_tn(v, dctx[:, cols])
            probs.append(prob.astype(BF))
            dscores.append((prob * (dprob - delta[:, cols])).astype(BF))
        dk, dv = None, None
        for n, i in enumerate(range(j, blocks)):
            cols = slice(i * BLK, (i + 1) * BLK)
            dv_term = dot_nt(dctx[:, cols], probs[n])
            dk_term = dot_nt(u_ref[0, 0, 0, :, cols], dscores[n])
            dv = dv_term if dv is None else dv + dv_term
            dk = dk_term if dk is None else dk + dk_term
            dq_term = dot_nn(k, dscores[n])
            if j == 0:
                dq_ref[:, cols] = dq_term
            else:
                dq_ref[:, cols] += dq_term
        out_ref[0, 1, 0, :, keys] = (dk * SCORE_SCALE).astype(BF)
        out_ref[0, 2, 0, :, keys] = dv.astype(BF)
    out_ref[0, 0, 0] = (dq_ref[...] * SCORE_SCALE).astype(BF)


def attend_back(units, starts, context, dcontext, lse):
    groups, _, heads = units.shape[:3]
    per_unit = pl.BlockSpec((1, 1, HD, SLOT), lambda g, h: (g, h, 0, 0))
    return pl.pallas_call(
        attend_back_kernel,
        grid=(groups, heads),
        out_shape=sds(units.shape, BF),
        in_specs=[
            pl.BlockSpec((1, 3, 1, HD, SLOT), lambda g, h: (g, 0, h, 0, 0)),
            pl.BlockSpec((1, 1, SLOT), lambda g, h: (g // 2, 0, 0)),
            per_unit,
            per_unit,
            pl.BlockSpec((1, 1, 1, SLOT), lambda g, h: (g, h, 0, 0)),
        ],
        out_specs=pl.BlockSpec((1, 3, 1, HD, SLOT), lambda g, h: (g, 0, h, 0, 0)),
        scratch_shapes=[pltpu.VMEM((HD, SLOT), F32)],
        compiler_params=params(),
        name="attend_back",
    )(units, starts, context, dcontext, lse)


def out_kernel(
    ctx_ref, wo_ref, tk_ref, vec_ref, ctxc_ref, resid_ref, n2_ref, half, part, got, xs, cs_s, cs_r
):
    dp, x, c = here()
    core = (dp, x * 2 + 1 - c)
    x_peer = (dp, (1 - x) * 2 + c)
    greet([core, x_peer])
    theirs = pl.ds(pl.multiple_of((1 - x) * HALF, HALF), HALF)
    ours = pl.ds(pl.multiple_of(x * HALF, HALF), HALF)
    cross = remote(ctx_ref.at[2, :, theirs], half, xs.at[0], xs.at[1], x_peer)
    cross.start()
    chunks = []

    def send(chunk, values):
        rows = rows_at(chunk * BLK, BLK)
        part[rows, :] = values.astype(BF)
        copy = remote(part.at[rows], got.at[rows], cs_s.at[chunk], cs_r.at[chunk], core)
        copy.start()
        chunks.append((chunk, copy))

    for i in range(SLOT // BLK):
        lanes = slice(i * BLK, (i + 1) * BLK)
        chunk = x * 2 + i
        out_lanes = rows_at(chunk * BLK, BLK)
        zero, one = ctx_ref[0, :, lanes], ctx_ref[1, :, lanes]
        send(chunk, dot_tt(zero, wo_ref[0]) + dot_tt(one, wo_ref[1]))
        ctxc_ref[0, :, out_lanes] = zero
        ctxc_ref[1, :, out_lanes] = one
    cross.wait()
    for i in range(HALF // BLK):
        chunk = (1 - x) * 4 + i
        out_lanes = rows_at(chunk * BLK, BLK)
        own = ctx_ref[2, :, rows_at(x * HALF + i * BLK, BLK)]
        other = half[:, i * BLK : (i + 1) * BLK]
        send(chunk, dot_tt(own, wo_ref[x]) + dot_tt(other, wo_ref[1 - x]))
        ctxc_ref[x, :, out_lanes] = own
        ctxc_ref[1 - x, :, out_lanes] = other
    for chunk, copy in chunks:
        copy.wait()
        rows = rows_at(chunk * BLK, BLK)
        tok = tk_ref[rows_at(x * HALF + chunk * BLK, BLK), :].astype(F32)
        summed = part[rows, :].astype(F32) + got[rows, :].astype(F32)
        resid = tok + summed + vec_ref[6:7, :]
        resid_ref[rows, :] = resid
        unit, _ = norm_parts(resid)
        n2_ref[rows, :] = (unit * vec_ref[2:3, :] + vec_ref[3:4, :]).astype(BF)


def project_out(ctx, wo, tk, vectors):
    cols = ctx.shape[1]
    width = tk.shape[1]
    rows = SLOT + HALF
    return pl.pallas_call(
        out_kernel,
        out_shape=(sds((2, cols, rows), BF), sds((rows, width), F32), sds((rows, width), BF)),
        in_specs=[VM] * 4,
        out_specs=(VM, VM, VM),
        scratch_shapes=[
            pltpu.VMEM((cols, HALF), BF),
            pltpu.VMEM((rows, width), BF),
            pltpu.VMEM((rows, width), BF),
            pltpu.SemaphoreType.DMA((2,)),
            pltpu.SemaphoreType.DMA((rows // BLK,)),
            pltpu.SemaphoreType.DMA((rows // BLK,)),
        ],
        compiler_params=params(3),
        name="out_norm",
    )(ctx, wo, tk, vectors)


GELU_C = math.sqrt(2.0 / math.pi)
GELU_A = 0.044715


def ffn_kernel(
    n2_ref, gl_ref, wf_ref, wp_ref, fb_ref, br_ref, dn2_ref, gf_ref, gp_ref, gb_ref, act, dpre
):
    rows_all, width = n2_ref.shape
    hidden = wf_ref.shape[2]

    def forward_back(i, carry):
        rows = rows_at(i * BLK, BLK)
        n2, gl = n2_ref[rows, :], gl_ref[rows, :]
        for s in range(2):
            lanes = slice(s * hidden, (s + 1) * hidden)
            u = dot_nn(n2, wf_ref[s]) + fb_ref[s]
            up = dot_nn(gl, wp_ref[s])
            t = jnp.tanh(GELU_C * (u + GELU_A * u * u * u))
            act[rows, lanes] = (0.5 * u * (1.0 + t)).astype(BF)
            slope = 0.5 * (1.0 + t) + 0.5 * u * (1.0 - t * t) * GELU_C * (
                1.0 + 3.0 * GELU_A * u * u
            )
            d = (up * slope).astype(BF)
            dpre[rows, lanes] = d
            gb_ref[s] += jnp.sum(d.astype(F32), axis=0, keepdims=True)
        br = dot_nt(act[rows, :hidden], wp_ref[0]) + dot_nt(act[rows, hidden:], wp_ref[1])
        br_ref[rows, :] = br.astype(BF)
        dn = dot_nt(dpre[rows, :hidden], wf_ref[0]) + dot_nt(dpre[rows, hidden:], wf_ref[1])
        dn2_ref[rows, :] = dn.astype(BF)
        return carry

    gb_ref[...] = jnp.zeros_like(gb_ref)
    lax.fori_loop(0, rows_all // BLK, forward_back, 0)
    for s in range(2):

        def weight_grads(i, carry, s=s):
            lanes = rows_at(i * BLK, BLK)
            wide = rows_at(s * hidden + i * BLK, BLK)
            gp_ref[s, :, lanes] = dot_tn(gl_ref[...], act[:, wide]).astype(BF)
            gf_ref[s, :, lanes] = dot_tn(n2_ref[...], dpre[:, wide]).astype(BF)
            return carry

        lax.fori_loop(0, hidden // BLK, weight_grads, 0)


def feed_forward(n2, gl, wf, wp, fb):
    rows, width = n2.shape
    hidden = wf.shape[2]
    return pl.pallas_call(
        ffn_kernel,
        out_shape=(
            sds((rows, width), BF),
            sds((rows, width), BF),
            sds(wf.shape, BF),
            sds(wp.shape, BF),
            sds((2, 1, hidden), F32),
        ),
        in_specs=[VM] * 5,
        out_specs=(VM,) * 5,
        scratch_shapes=[
            pltpu.VMEM((rows, 2 * hidden), BF),
            pltpu.VMEM((rows, 2 * hidden), BF),
        ],
        compiler_params=params(),
        name="feed_forward",
    )(n2, gl, wf, wp, fb)


def mid_kernel(
    br_ref, dn_ref, resid_ref, gl_ref, ctxc_ref, wo_ref, vec_ref,
    mixed_ref, dres_ref, dctx_ref, go_ref, vg_ref,
    low, got_br, got_dn, outgoing, half, bs, xs, cs_s, cs_r,
):
    dp, x, c = here()
    core = (dp, x * 2 + 1 - c)
    x_peer = (dp, (1 - x) * 2 + c)
    greet([core, x_peer])
    rows_all, width = dn_ref.shape
    own_rows = rows_all // 2
    their = pl.ds(pl.multiple_of((1 - c) * own_rows, BLK), own_rows)
    n_chunks = rows_all // BLK
    copies = []
    for r in range(n_chunks):
        rows = pl.ds(r * BLK, BLK)
        copy = remote(dn_ref.at[rows], got_dn.at[rows], cs_s.at[r], cs_r.at[r], core)
        copy.start()
        copies.append(copy)
    branch = remote(br_ref.at[their], got_br, bs.at[0], bs.at[1], core)
    branch.start()
    vg_ref[...] = jnp.zeros_like(vg_ref)
    gain = vec_ref[2:3, :]
    for r in range(n_chunks):
        copies[r].wait()
        rows = slice(r * BLK, (r + 1) * BLK)
        dn = dn_ref[rows, :].astype(F32) + got_dn[rows, :].astype(F32)
        unit, scale = norm_parts(resid_ref[rows, :])
        e = dn * gain
        dres = gl_ref[rows, :].astype(F32) + scale * (
            e
            - jnp.mean(e, axis=-1, keepdims=True)
            - unit * jnp.mean(e * unit, axis=-1, keepdims=True)
        )
        low[rows, :] = dres.astype(BF)
        dres_ref[rows, :] = dres

        @pl.when(c == r // (n_chunks // 2))
        def _(dn=dn, unit=unit, dres=dres):
            vg_ref[0:1, :] += jnp.sum(dn * unit, axis=0, keepdims=True)
            vg_ref[1:2, :] += jnp.sum(dn, axis=0, keepdims=True)
            vg_ref[2:3, :] += jnp.sum(dres, axis=0, keepdims=True)

    for i in range(HALF // BLK):
        lanes = slice(i * BLK, (i + 1) * BLK)
        rows = rows_at((1 - x) * SLOT + i * BLK, BLK)
        outgoing[:, lanes] = dot_tt(wo_ref[1 - x], low[rows, :]).astype(BF)
        dctx_ref[2, :, rows_at(x * HALF + i * BLK, BLK)] = dot_tt(
            wo_ref[x], low[rows, :]
        ).astype(BF)
    cross = remote(outgoing, half, xs.at[0], xs.at[1], x_peer)
    cross.start()
    for i in range(SLOT // BLK):
        lanes = slice(i * BLK, (i + 1) * BLK)
        rows = rows_at(x * HALF + i * BLK, BLK)
        for s in range(2):
            dctx_ref[s, :, lanes] = dot_tt(wo_ref[s], low[rows, :]).astype(BF)
    for s in range(2):
        go_ref[s] = dot_tt(low[...], ctxc_ref[s]).astype(BF)
    branch.wait()
    for r in range(own_rows // BLK):
        rows = slice(r * BLK, (r + 1) * BLK)
        wide = rows_at(c * own_rows + r * BLK, BLK)
        mixed = (
            resid_ref[wide, :]
            + br_ref[wide, :].astype(F32)
            + got_br[rows, :].astype(F32)
            + vec_ref[7:8, :]
        )
        mixed_ref[rows, :] = mixed.astype(BF)
        vg_ref[3:4, :] += jnp.sum(gl_ref[wide, :].astype(F32), axis=0, keepdims=True)
    cross.wait()
    dctx_ref[2, :, pl.ds(pl.multiple_of((1 - x) * HALF, HALF), HALF)] = half[...]


def middle_back(br, dn, resid, gl, ctxc, wo, vectors):
    rows, width = dn.shape
    cols = ctxc.shape[1]
    return pl.pallas_call(
        mid_kernel,
        out_shape=(
            sds((rows // 2, width), BF),
            sds((rows, width), F32),
            sds((3, cols, SLOT), BF),
            sds((2, width, cols), BF),
            sds((8, width), F32),
        ),
        in_specs=[VM] * 7,
        out_specs=(VM,) * 5,
        scratch_shapes=[
            pltpu.VMEM((rows, width), BF),
            pltpu.VMEM((rows // 2, width), BF),
            pltpu.VMEM((rows, width), BF),
            pltpu.VMEM((cols, HALF), BF),
            pltpu.VMEM((cols, HALF), BF),
            pltpu.SemaphoreType.DMA((2,)),
            pltpu.SemaphoreType.DMA((2,)),
            pltpu.SemaphoreType.DMA((rows // BLK,)),
            pltpu.SemaphoreType.DMA((rows // BLK,)),
        ],
        compiler_params=params(4),
        name="middle_back",
    )(br, dn, resid, gl, ctxc, wo, vectors)


def first_kernel(
    du_ref, n1_ref, wq_ref, dres_ref, tk_ref, vec_ref,
    gq_ref, ig_ref, vg_ref, qb_ref,
    half, part, got, xs, cs_s, cs_r,
):
    dp, x, c = here()
    core = (dp, x * 2 + 1 - c)
    x_peer = (dp, (1 - x) * 2 + c)
    greet([core, x_peer])
    cols = du_ref.shape[1]
    rows_all = SLOT + HALF
    own_chunks = rows_all // BLK // 2
    theirs = pl.ds(pl.multiple_of((1 - x) * HALF, HALF), HALF)
    cross = remote(du_ref.at[2, :, theirs], half, xs.at[0], xs.at[1], x_peer)
    cross.start()
    full_rows = pl.ds(pl.multiple_of(x * SLOT, SLOT), SLOT)
    part_rows = pl.ds(pl.multiple_of((1 - x) * SLOT, SLOT), SLOT)

    def send(chunk, values):
        part[rows_at(chunk * BLK, BLK), :] = values.astype(BF)

    for i in range(SLOT // BLK):
        lanes = slice(i * BLK, (i + 1) * BLK)
        send(
            x * 2 + i,
            dot_tt(du_ref[0, :, lanes], wq_ref[0]) + dot_tt(du_ref[1, :, lanes], wq_ref[1]),
        )
    cross.wait()
    for i in range(HALF // BLK):
        own = du_ref[2, :, rows_at(x * HALF + i * BLK, BLK)]
        send(
            (1 - x) * 4 + i,
            dot_tt(own, wq_ref[x]) + dot_tt(half[:, i * BLK : (i + 1) * BLK], wq_ref[1 - x]),
        )
    their = pl.ds(pl.multiple_of((1 - c) * own_chunks * BLK, BLK), own_chunks * BLK)
    swap = remote(part.at[their], got, cs_s, cs_r, core)
    swap.start()
    ones = jnp.ones((8, SLOT), BF)
    for s in range(2):
        gq_ref[s] = dot_tt(n1_ref[full_rows, :], du_ref[s]).astype(BF)
    gq_ref[x] = (
        gq_ref[x].astype(F32) + dot_tt(n1_ref[part_rows, :], du_ref[2])
    ).astype(BF)
    for g in range(3):
        qb_ref[g] = dot_nt(ones, du_ref[g])
    swap.wait()
    vg_ref[...] = jnp.zeros_like(vg_ref)
    gain = vec_ref[0:1, :]
    for r in range(own_chunks):
        rows = slice(r * BLK, (r + 1) * BLK)
        wide = rows_at((c * own_chunks + r) * BLK, BLK)
        tok_rows = rows_at(x * HALF + (c * own_chunks + r) * BLK, BLK)
        dn = part[wide, :].astype(F32) + got[rows, :].astype(F32)
        unit, scale = norm_parts(tk_ref[tok_rows, :].astype(F32))
        e = dn * gain
        back = scale * (
            e
            - jnp.mean(e, axis=-1, keepdims=True)
            - unit * jnp.mean(e * unit, axis=-1, keepdims=True)
        )
        ig_ref[rows, :] = (dres_ref[wide, :] + back).astype(BF)
        vg_ref[0:1, :] += jnp.sum(dn * unit, axis=0, keepdims=True)
        vg_ref[1:2, :] += jnp.sum(dn, axis=0, keepdims=True)


def first_back(du, n1, wq, dres, tk, vectors):
    cols = du.shape[1]
    width = tk.shape[1]
    rows = SLOT + HALF
    return pl.pallas_call(
        first_kernel,
        out_shape=(
            sds((2, width, cols), BF),
            sds((rows // 2, width), BF),
            sds((8, width), F32),
            sds((3, 8, cols), F32),
        ),
        in_specs=[VM] * 6,
        out_specs=(VM,) * 4,
        scratch_shapes=[
            pltpu.VMEM((cols, HALF), BF),
            pltpu.VMEM((rows, width), BF),
            pltpu.VMEM((rows // 2, width), BF),
            pltpu.SemaphoreType.DMA((2,)),
            pltpu.SemaphoreType.DMA,
            pltpu.SemaphoreType.DMA,
        ],
        compiler_params=params(5),
        name="first_back",
    )(du, n1, wq, dres, tk, vectors)


def reduce_kernel(n, *refs):
    grads = refs[:n]
    vec_ref = refs[n]
    sums = refs[n + 1 : 2 * n + 1]
    vec_out, sq_out = refs[2 * n + 1 : 2 * n + 3]
    rest = refs[2 * n + 3 :]
    r1x, r1y, r2x, r2y, r3, s3, m1, m2 = (rest[i * n : (i + 1) * n] for i in range(8))
    vgot, sgot, ss, rs, vs_s, vs_r, qs_s, qs_r = rest[8 * n :]
    dp, x, c = here()
    z, y = dp // 2, dp % 2
    me = x * 2 + c
    z_peers = [(lax.rem(z + k, 4) * 2 + y, me) for k in (1, 2, 3)]
    x_peer = (dp, (1 - x) * 2 + c)
    y_peer = (z * 2 + 1 - y, me)
    core = (dp, x * 2 + 1 - c)
    greet(z_peers + [x_peer, y_peer, core])
    first, early, second, third = [], [], [], []
    for a in range(n):
        g = grads[a]
        first.append(
            [
                remote(g.at[1 - x, pl.ds(0, 2), 1 - y], r1y[a], ss.at[a, 0], rs.at[a, 0], y_peer),
                remote(g.at[1 - x, pl.ds(2, 2), 1 - y], r1x[a], ss.at[a, 1], rs.at[a, 1], x_peer),
            ]
        )
        early.append(
            [
                remote(
                    g.at[1 - x, pl.ds(2, 2), y],
                    r2x[a].at[pl.ds(2, 2)],
                    ss.at[a, 7],
                    rs.at[a, 7],
                    x_peer,
                ),
                remote(
                    g.at[x, pl.ds(0, 2), 1 - y],
                    r2y[a].at[pl.ds(0, 2)],
                    ss.at[a, 8],
                    rs.at[a, 8],
                    y_peer,
                ),
            ]
        )
        second.append(
            [
                remote(m1[a], r2x[a].at[pl.ds(0, 2)], ss.at[a, 2], rs.at[a, 2], x_peer),
                remote(m2[a], r2y[a].at[pl.ds(2, 2)], ss.at[a, 3], rs.at[a, 3], y_peer),
            ]
        )
        third.append(
            [
                remote(s3[a].at[k], r3[a].at[k], ss.at[a, 4 + k], rs.at[a, 4 + k], z_peers[k])
                for k in range(3)
            ]
        )

    def all_sum(value_ref, got, send, recv):
        for i, peers in enumerate(([core], [x_peer], [y_peer], z_peers)):
            base = i if i < 3 else 3
            copies = [
                remote(value_ref, got.at[base + k], send.at[base + k], recv.at[base + k], peer)
                for k, peer in enumerate(peers)
            ]
            for one in copies:
                one.start()
            for one in copies:
                one.wait()
            if len(peers) == 1:
                value_ref[...] += got[base]
            else:
                blocks = [value_ref[...]] + [got[base + k] for k in range(3)]
                total = None
                for place in range(4):
                    term = blocks[0]
                    for k in range(1, 4):
                        term = jnp.where(lax.rem(z + 4 - k, 4) == place, blocks[k], term)
                    total = term if total is None else total + term
                value_ref[...] = total

    def stage_two(a):
        for one in first[a]:
            one.wait()
        for k in range(2):
            m1[a][k] = (grads[a][1 - x, k, y].astype(F32) + r1y[a][k].astype(F32)).astype(BF)
            m2[a][k] = (grads[a][x, 2 + k, 1 - y].astype(F32) + r1x[a][k].astype(F32)).astype(BF)
        for one in second[a]:
            one.start()

    def column(a, place):
        return (
            grads[a][x, place, y].astype(F32)
            + r2x[a][place].astype(F32)
            + r2y[a][place].astype(F32)
        )

    def stage_three(a):
        for one in early[a] + second[a]:
            one.wait()
        for k in range(3):
            s3[a][k] = column(a, lax.rem(z + k + 1, 4)).astype(BF)
            third[a][k].start()
        sums[a][...] = column(a, z)

    for a in range(n):
        for one in first[a] + early[a]:
            one.start()
    vec_out[...] = vec_ref[...]
    for a in range(n):
        stage_two(a)
        if a > 0:
            stage_three(a - 1)
    stage_three(n - 1)
    all_sum(vec_out, vgot, vs_s, vs_r)
    squares = jnp.zeros((), F32)
    for a in range(n):
        for one in third[a]:
            one.wait()
        total = (
            sums[a][...]
            + r3[a][0].astype(F32)
            + r3[a][1].astype(F32)
            + r3[a][2].astype(F32)
        )
        sums[a][...] = total
        squares = squares + jnp.sum(total * total)
    sq_out[...] = jnp.full(sq_out.shape, squares, F32)
    all_sum(sq_out, sgot, qs_s, qs_r)


def reduce_grads(grads, vec):
    n = len(grads)
    if lax.axis_size("dp") != 8:
        slot = lax.axis_index("tensor") // 2
        swap = [(0, 2), (1, 3), (2, 0), (3, 1)]
        sums = []
        for g in grads:
            mine = jnp.where(slot == 0, g[0], g[1])
            other = jnp.where(slot == 0, g[1], g[0])
            total = mine.astype(F32) + lax.ppermute(other, "tensor", swap).astype(F32)
            sums.append(
                lax.psum_scatter(total.astype(BF), "dp", scatter_dimension=0, tiled=True).astype(F32)
            )
        squares = sum(jnp.sum(s * s) for s in sums)
        vec, squares = lax.psum((vec, squares), ("dp", "tensor"))
        return sums, vec, squares
    shapes = [(g.shape[1] // 8, g.shape[2]) for g in grads]
    wide = [g.reshape((2, 4, 2) + s) for g, s in zip(grads, shapes, strict=True)]
    scratch = []
    for lead in (2, 2, 4, 4, 3, 3, 2, 2):
        scratch += [pltpu.VMEM((lead,) + s, BF) for s in shapes]
    outs = pl.pallas_call(
        functools.partial(reduce_kernel, n),
        out_shape=tuple(sds(s, F32) for s in shapes)
        + (sds(vec.shape, F32), sds((8, 128), F32)),
        in_specs=[VM] * (n + 1),
        out_specs=(VM,) * (n + 2),
        scratch_shapes=scratch
        + [
            pltpu.VMEM((6,) + vec.shape, F32),
            pltpu.VMEM((6, 8, 128), F32),
            pltpu.SemaphoreType.DMA((n, 9)),
            pltpu.SemaphoreType.DMA((n, 9)),
            pltpu.SemaphoreType.DMA((6,)),
            pltpu.SemaphoreType.DMA((6,)),
            pltpu.SemaphoreType.DMA((6,)),
            pltpu.SemaphoreType.DMA((6,)),
        ],
        compiler_params=params(6),
        name="reduce_grads",
    )(*wide, vec)
    return list(outs[:n]), outs[n], outs[n + 1][0, 0]


def adamw_update(weight, moment_one, moment_two, gradient, step_rate, decay_rate):
    first_moment = DECAY_FIRST * moment_one + (1.0 - DECAY_FIRST) * gradient
    second_moment = DECAY_SECOND * moment_two + (1.0 - DECAY_SECOND) * gradient * gradient
    first_hat = first_moment / (1.0 - DECAY_FIRST**STEP)
    second_hat = second_moment / (1.0 - DECAY_SECOND**STEP)
    fresh_weight = weight - step_rate * (
        first_hat / (jnp.sqrt(second_hat) + ADAM_EPSILON) + decay_rate * weight
    )
    return (fresh_weight, first_moment, second_moment)


def on_device(
    tokens,
    cotangent,
    segment_ids,
    valid,
    qkv_weight,
    qkv_moment1,
    qkv_moment2,
    out_weight,
    out_moment1,
    out_moment2,
    fc_weight,
    fc_moment1,
    fc_moment2,
    proj_weight,
    proj_moment1,
    proj_moment2,
    vector_params,
    vector_moment1,
    vector_moment2,
    fc_bias,
    fc_bias_moment1,
    fc_bias_moment2,
):
    tensor_count = lax.axis_size("tensor")
    rank = lax.axis_index("tensor")
    x, c = rank // 2, rank % 2
    width = vector_params.shape[1]
    cols = width // tensor_count
    heads = cols // HD
    hidden = fc_bias.shape[0] // tensor_count
    part_rows = qkv_weight.shape[0]

    wq_s = qkv_weight.reshape(part_rows, 3 * cols).astype(BF)
    wo_s = out_weight.T.astype(BF)
    wf_s = fc_weight.astype(BF)
    wp_s = proj_weight.T.astype(BF)
    grad_low = cotangent * valid.astype(BF)[:, None]

    rows3 = segment_ids.reshape(-1, SLOT)
    starts = jnp.sum((rows3[:, None, :] < rows3[:, :, None]).astype(jnp.int32), axis=-1)
    starts = jnp.stack([lax.dynamic_index_in_dim(starts, 2 * x, 0, False), starts[1]])[:, None, :]

    def of_slots(vector):
        parts = vector.reshape(tensor_count, -1)
        return jnp.stack([lax.dynamic_index_in_dim(parts, c + 2 * s, 0, False) for s in range(2)])

    qb, vb = of_slots(vector_params[4]), of_slots(vector_params[5])
    bias = jnp.concatenate([qb, jnp.zeros_like(qb), vb], axis=1)[:, :, None]
    fb = of_slots(fc_bias)[:, None, :]

    tk, gl = share_tokens(tokens, grad_low)
    wq, wo, wf, wp = gather_weights([wq_s, wo_s, wf_s, wp_s])
    n1, u = project_qkv(tk, vector_params, bias, wq)
    units = u.reshape(3, 3, heads, HD, SLOT)
    ctx, lse = attend(units, starts)
    ctxc, resid, n2 = project_out(ctx.reshape(3, cols, SLOT), wo, tk, vector_params)
    br, dn, gf, gp, gb = feed_forward(n2, gl, wf, wp, fb)
    mixed, dres, dctx, go, vg2 = middle_back(br, dn, resid, gl, ctxc, wo, vector_params)
    du = attend_back(units, starts, ctx, dctx.reshape(ctx.shape), lse)
    gq, input_grad, vg1, qb_sums = first_back(
        du.reshape(u.shape), n1, wq, dres, tk, vector_params
    )
    sums = qb_sums[:, 0, :]
    own_slot = (jnp.arange(2) == x).astype(F32)[:, None]
    per_slot = sums[:2] + own_slot * sums[2:3]

    def to_heads(values):
        return lax.dynamic_update_slice(
            lax.dynamic_update_slice(
                jnp.zeros((tensor_count, values.shape[1]), F32), values[:1], (c, 0)
            ),
            values[1:],
            (c + 2, 0),
        )

    vec = jnp.concatenate(
        [
            vg1[:2],
            vg2[:2],
            to_heads(per_slot[:, :cols]).reshape(1, width),
            to_heads(per_slot[:, 2 * cols :]).reshape(1, width),
            vg2[2:4],
            to_heads(gb[:, 0, :]).reshape(-1, width),
        ],
        axis=0,
    )
    n_vec = vec.shape[0]
    vec = jnp.pad(vec, ((0, -n_vec % 8), (0, 0)))
    (gq, go, gf, gp), vec, squares = reduce_grads([gq, go, gf, gp], vec)
    vec = vec[:n_vec]
    vector_grad, fc_bias_grad = vec[:8], vec[8:].reshape(-1)
    grad_norm = jnp.sqrt(squares + jnp.sum(vec * vec))
    factor = CLIP_NORM / jnp.maximum(grad_norm, CLIP_NORM)
    qkv_new = adamw_update(
        qkv_weight, qkv_moment1, qkv_moment2, factor * gq.reshape(qkv_weight.shape), RATE_MATRIX, WEIGHT_DECAY
    )
    out_new = adamw_update(
        out_weight, out_moment1, out_moment2, factor * go.T, RATE_MATRIX, WEIGHT_DECAY
    )
    fc_new = adamw_update(fc_weight, fc_moment1, fc_moment2, factor * gf, RATE_MATRIX, WEIGHT_DECAY)
    proj_new = adamw_update(
        proj_weight, proj_moment1, proj_moment2, factor * gp.T, RATE_MATRIX, WEIGHT_DECAY
    )
    vector_new = adamw_update(
        vector_params, vector_moment1, vector_moment2, factor * vector_grad, RATE_VECTOR, 0.0
    )
    fc_bias_new = adamw_update(
        fc_bias, fc_bias_moment1, fc_bias_moment2, factor * fc_bias_grad, RATE_VECTOR, 0.0
    )
    return (
        mixed,
        input_grad,
        grad_norm,
        *qkv_new,
        *out_new,
        *fc_new,
        *proj_new,
        *vector_new,
        *fc_bias_new,
    )


def solution(mesh):
    rows = P(("dp", "tensor"), None)
    by_rows = [P("dp", None, "tensor")] * 3
    by_out = [P("tensor", "dp")] * 3
    by_fc = [P("dp", "tensor")] * 3
    weights = by_rows + by_out + by_fc + by_out
    return jax.shard_map(
        on_device,
        mesh=mesh,
        in_specs=(rows, rows, P("dp"), P(("dp", "tensor")), *weights, *[P()] * 6),
        out_specs=(rows, rows, P(), *weights, *[P()] * 6),
        check_vma=False,
    )
```

time: 817 us -> 466 us (0.57)
  Pallas kernels: 0 us -> 421 us
  waiting for transfers between devices: 320 us -> 0 us
  matrix products: 172 us -> 0 us
  blocking collectives: 108 us -> 0 us
  other arithmetic: 97.2 us -> 14.3 us
  local copies, waits for them, and re-layouts: 66.1 us -> 18 us
  starting transfers between devices: 19.9 us -> 0 us
  between operations: 22.2 us -> 4 us
    pallas_call x0 -> x10, Pallas kernels: none -> 421 us  [the longest x1 117 us: reduce_grads(): pl.pallas_call(functools.partial(reduce_kernel, n), out_shape=tuple((sds(...]
    dot_general x33 -> x0, matrix products: 172 us -> none  [the longest x3 24.4 us: attend_back(): jnp.einsum('qhe,khe->hqk', dcontext_rows, value_rows, preferred_element_t...]
    all_gather x6 -> x0, waiting for transfers between devices: 142 us -> none  [the longest x1 38 us: on_device(): grad_rows = lax.all_gather(grad_low, 'tensor', axis=0, tiled=True)]
    reduce_scatter x4 -> x0, waiting for transfers between devices: 123 us -> none  [the longest x1 45.3 us: on_device(): lax.psum_scatter(jnp.dot(context, out_local, preferred_element_type=jnp.f...]
    all_gather x2 -> x0, blocking collectives: 70 us -> none  [the longest x1 38.9 us: on_device(): lax.all_gather(qkv_weight.astype(jnp.bfloat16), 'dp', axis=0, tiled=True)]
    all_to_all x4 -> x0, waiting for transfers between devices: 54.5 us -> none  [sum_at_owner(): lax.all_to_all(cut_along(shard, dim, devices), axis, 0, 0, tiled=True)]
    psum x1 -> x0, blocking collectives: 37.7 us -> none  [on_device(): matrix_squares = lax.psum(local_squares, ('dp', 'tensor'))]
    reduce_sum x24 -> x2, other arithmetic: 40.3 us -> 3.12 us  [the longest x1 1.7 us: on_device(): jnp.sum((rows3[:, None, :] < rows3[:, :, None]).astype(jnp.int32), axis=-1)]
  transfers between devices with their start and end apart: 14 -> 0, of which waited for: 11 -> 0; matrix products, arithmetic and copies ran while one was open for 12% -> 0% of each run, Pallas kernels for 0% -> 0%
where the time goes in v1:
time: 466 us; the launch traced here: 457 us
  Pallas kernels  421 us (90%)
  local copies, waits for them, and re-layouts  18 us (4%)
  other arithmetic  14.3 us (3%)
    pallas_call x1, Pallas kernels, reduce_grads(): pl.pallas_call(functools.partial(reduce_kernel, n), out_shape=tuple((sds(...  117 us
    pallas_call x1, Pallas kernels, gather_weights(): pl.pallas_call(functools.partial(gather_kernel, n), out_shape=tuple((sds(...  79.2 us
    pallas_call x1, Pallas kernels, share_tokens(): pl.pallas_call(share_kernel, out_shape=(sds((2 * SLOT, width), BF), sds((...  75.6 us
    pallas_call x1, Pallas kernels, feed_forward(): pl.pallas_call(ffn_kernel, out_shape=(sds((rows, width), BF), sds((rows,...  33.2 us
    pallas_call x1, Pallas kernels, first_back(): pl.pallas_call(first_kernel, out_shape=(sds((2, width, cols), BF), sds((r...  30.4 us
    pallas_call x1, Pallas kernels, middle_back(): pl.pallas_call(mid_kernel, out_shape=(sds((rows // 2, width), BF), sds((r...  21.8 us
    pallas_call x1, Pallas kernels, attend_back(): pl.pallas_call(attend_back_kernel, grid=(groups, heads), out_shape=sds(un...  19.9 us
    pallas_call x1, Pallas kernels, attend(): pl.pallas_call(attend_kernel, grid=(groups, heads), out_shape=(sds((group...  17.4 us

profile of v1, /device:TPU:0, one launch (start us, length us, event | category | flops | bytes accessed | tf_op | source)
XLA Modules:
  0.0 457.2 jit_solution(8444693477841541344)
XLA Ops:
  0.7 0.7 convert_element_type.33
  1.3 2.5 broadcast_multiply_fusion.grad_ref
  3.9 75.6 %share_tokens.1 = (bf16[2048,768]{1,0:T(8,128)(2,1)}, bf16[1536,768]{1,0:T(8,128)(2,1)}) custom-call(bf16[768,768]{1,0:T(8,128)(2,1)} %tok_ref.1, bf16[768,768]{1,0:T(8,128)(2,1)} %broadcast_multiply_fusion.grad_ref), custom_call_target="tpu_custom_call" | custom-call | tf_op jit(solution)/shard_map/share_tokens/pallas_call | solution.py:143
  79.5 0.8 slice_reduce_fusion.1
  80.3 0.1 reshape_squeeze.7
  80.4 0.1 reshape_squeeze.6
  80.5 0.1 pad.11.clone
  80.6 1.1 copy.76.bias_ref
  81.7 0.2 copy.73
  81.8 0.8 copy.75.refs_0_
  82.6 0.1 copy.74
  82.7 0.6 convert_bitcast_fusion.1.refs_1_
  83.3 0.7 convert_element_type.38.refs_2_
  84.0 0.7 convert_bitcast_fusion.refs_3_
  84.7 79.2 %gather_weights.1 = (bf16[2,4,2,96,576]{4,3,2,1,0:T(8,128)(2,1)}, bf16[2,4,2,96,192]{4,3,2,1,0:T(8,128)(2,1)}, bf16[2,4,2,96,768]{4,3,2,1,0:T(8,128)(2,1)}, bf16[2,4,2,96,768]{4,3,2,1,0:T(8,128)(2,1)}) custom-call(bf16[96,576]{1,0:T(8,128)(2,1)} %copy.75.refs_0_, bf16[96,192]{1,0:T(8,128)(2,1)} %convert_bitcast_fusion.1.refs_1_, ...), custom_call_target="tpu_custom_call" | custom-call | tf_op jit(solution)/shard_map/gather_weights/pallas_call | solution.py:225
  163.9 0.0 copy-start.18
  163.9 11.5 %norm_qkv.1 = (bf16[2048,768]{1,0:T(8,128)(2,1)}, bf16[3,576,1024]{2,1,0:T(8,128)(2,1)}) custom-call(bf16[2048,768]{1,0:T(8,128)(2,1)} %get-tuple-element.54.tk_ref, f32[8,768]{1,0:T(8,128)} %vec_ref.7, f32[2,576,1]{2,1,0:T(8,128)} %copy.76.bias_ref, bf16[2,768,576]{2,1,0:T(8,128)(2,1)} %bitcast.40), custom_call_target="tpu_custom_call" | custom-call | tf_op jit(solution)/shard_map/norm_qkv/pallas_call | solution.py:267
  175.4 1.7 convert_reduce_fusion
  177.2 0.6 broadcast_in_dim.19.start_ref
  177.8 17.4 %attend.1 = (bf16[3,3,64,1024]{3,2,1,0:T(8,128)(2,1)}, f32[3,3,1,1024]{3,2,1,0:T(1,128)}) custom-call(bf16[3,3,3,64,1024]{4,3,2,1,0:T(8,128)(2,1)} %bitcast.37, s32[2,1,1024]{2,1,0:T(1,128)} %broadcast_in_dim.19.start_ref), custom_call_target="tpu_custom_call" | custom-call | tf_op jit(solution)/shard_map/attend/pallas_call | solution.py:318
  195.2 15.0 %out_norm.1 = (bf16[2,192,1536]{2,1,0:T(8,128)(2,1)}, f32[1536,768]{1,0:T(8,128)}, bf16[1536,768]{1,0:T(8,128)(2,1)}) custom-call(bf16[3,192,1024]{2,1,0:T(8,128)(2,1)} %bitcast.42, bf16[2,768,192]{2,1,0:T(8,128)(2,1)} %bitcast.43, bf16[2048,768]{1,0:T(8,128)(2,1)} %get-tuple-element.54.tk_ref, f32[8,768]{1,0:T(8,128)} %vec_ref.7), custom_call_target="tpu_custom_call" | custom-call | tf_op jit(solution)/shard_map/out_norm/pallas_call | solution.py:443
  210.3 0.6 broadcast_in_dim.20.fb_ref
  210.9 33.2 %feed_forward.1 = (bf16[1536,768]{1,0:T(8,128)(2,1)}, bf16[1536,768]{1,0:T(8,128)(2,1)}, bf16[2,768,768]{2,1,0:T(8,128)(2,1)}, bf16[2,768,768]{2,1,0:T(8,128)(2,1)}, f32[2,1,768]{2,1,0:T(1,128)}) custom-call(bf16[1536,768]{1,0:T(8,128)(2,1)} %get-tuple-element.59.n2_ref, bf16[1536,768]{1,0:T(8,128)(2,1)} %get-tuple-element.60.gl_ref, ...), custom_call_target="tpu_custom_call" | custom-call | tf_op jit(solution)/shard_map/feed_forward/pallas_call | solution.py:509
  244.2 21.8 %middle_back.1 = (bf16[768,768]{1,0:T(8,128)(2,1)}, f32[1536,768]{1,0:T(8,128)}, bf16[3,192,1024]{2,1,0:T(8,128)(2,1)}, bf16[2,768,192]{2,1,0:T(8,128)(2,1)}, f32[8,768]{1,0:T(8,128)}) custom-call(bf16[1536,768]{1,0:T(8,128)(2,1)} %get-tuple-element.63.br_ref, bf16[1536,768]{1,0:T(8,128)(2,1)} %get-tuple-element.64.dn_ref, ...), custom_call_target="tpu_custom_call" | custom-call | tf_op jit(solution)/shard_map/middle_back/pallas_call | solution.py:607
  266.0 19.9 %attend_back.1 = bf16[3,3,3,64,1024]{4,3,2,1,0:T(8,128)(2,1)} custom-call(bf16[3,3,3,64,1024]{4,3,2,1,0:T(8,128)(2,1)} %bitcast.38, s32[2,1,1024]{2,1,0:T(1,128)} %broadcast_in_dim.19.start_ref, bf16[3,3,64,1024]{3,2,1,0:T(8,128)(2,1)} %get-tuple-element.57.ctx_ref, bf16[3,3,64,1024]{3,2,1,0:T(8,128)(2,1)} %bitcast.50, ...), custom_call_target="tpu_custom_call" | custom-call | tf_op jit(solution)/shard_map/attend_back/pallas_call | solution.py:373
  285.9 30.4 %first_back.1 = (bf16[2,768,576]{2,1,0:T(8,128)(2,1)}, bf16[768,768]{1,0:T(8,128)(2,1)}, f32[8,768]{1,0:T(8,128)}, f32[3,8,576]{2,1,0:T(8,128)}) custom-call(bf16[3,576,1024]{2,1,0:T(8,128)(2,1)} %bitcast.39, bf16[2048,768]{1,0:T(8,128)(2,1)} %get-tuple-element.70.n1_ref, bf16[2,768,576]{2,1,0:T(8,128)(2,1)} %bitcast.41, ...), custom_call_target="tpu_custom_call" | custom-call | tf_op jit(solution)/shard_map/first_back/pallas_call | solution.py:703
  316.3 0.7 slice.78
  317.0 0.8 slice.80
  317.8 0.7 slice_reduce_fusion.2
  318.6 0.1 bitcast_add_fusion
  318.7 0.1 reshape.121
  318.9 0.1 reshape.122
  319.0 0.1 dynamic_update_slice.22
  319.1 0.3 dynamic_update_slice.23
  319.4 0.1 concatenate.7
  319.4 0.6 pad.4.refs_4_
  320.1 116.8 %reduce_grads.1 = (f32[96,576]{1,0:T(8,128)}, f32[96,192]{1,0:T(8,128)}, f32[96,768]{1,0:T(8,128)}, f32[96,768]{1,0:T(8,128)}, f32[16,768]{1,0:T(8,128)}, /*index=5*/f32[8,128]{1,0:T(8,128)}) custom-call(bf16[2,4,2,96,576]{4,3,2,1,0:T(8,128)(2,1)} %bitcast.49, bf16[2,4,2,96,192]{4,3,2,1,0:T(8,128)(2,1)} %bitcast.52, bf16[2,4,2,96,768]{4,3,2,1,0:T(8,128)(2,1)} %bitcast.45, ...), custom_call_target="tpu_custom_call" | custom-call | tf_op jit(solution)/shard_map/reduce_grads/pallas_call | solution.py:876
  436.9 0.0 copy-start.10
  436.9 1.2 slice.92
  438.1 1.4 multiply_reduce_fusion
  440.9 0.1 copy.81
  441.1 1.0 broadcast_multiply_fusion.1
  442.1 0.1 copy.78
  442.2 0.1 copy.77
  442.4 0.0 copy-start.14
  442.4 0.1 copy.79
  442.6 0.2 multiply_subtract_fusion.2
  442.8 0.9 copy.86
  443.7 0.9 copy.87
  444.6 0.9 copy.88
  445.5 0.1 copy.82
  445.5 1.0 copy.83
  446.5 0.1 multiply_subtract_fusion.3
  446.7 0.0 copy-start.16
  446.7 0.0 copy-start.17
  446.7 0.7 copy.89
  447.4 0.7 copy.90
  448.2 0.7 copy.91
  448.9 1.1 multiply_subtract_fusion.1
  450.0 2.3 multiply_subtract_fusion
  452.3 0.6 multiply_subtract_fusion.4
  453.0 0.6 multiply_subtract_fusion.5
  453.6 1.0 copy.103
  454.6 1.0 copy.104
  (64 shorter events, 0.4 us)
Async XLA Ops:
  1.3 80.3 %copy-start.4 = (f32[96,3,192]{2,0,1:T(8,128)S(1)}, f32[96,3,192]{2,0,1:T(8,128)}, u32[]{:S(2)}) copy-start(f32[96,3,192]{2,0,1:T(8,128)} %param.26) | copy-start | bytes 663556
  3.8 78.8 %copy-start.13 = (f32[192,96]{1,0:T(8,128)S(1)}, f32[192,96]{1,0:T(8,128)}, u32[]{:S(2)}) copy-start(f32[192,96]{1,0:T(8,128)} %param.29) | copy-start | bytes 221188
  3.9 79.5 %copy-start = (f32[96,768]{1,0:T(8,128)S(1)}, f32[96,768]{1,0:T(8,128)}, u32[]{:S(2)}) copy-start(f32[96,768]{1,0:T(8,128)} %param.32) | copy-start | bytes 884740
  3.9 80.2 %copy-start.1 = (f32[768,96]{0,1:T(8,128)S(1)}, f32[768,96]{0,1:T(8,128)}, u32[]{:S(2)}) copy-start(f32[768,96]{0,1:T(8,128)} %param.35) | copy-start | bytes 884740
  163.9 11.5 %copy-start.18 = (s32[3072]{0:T(1024)S(1)}, s32[3072]{0:T(1024)}, u32[]{:S(2)}) copy-start(s32[3072]{0:T(1024)} %param.24) | copy-start | bytes 36868
  195.2 15.1 %copy-start.15 = (f32[3072]{0:T(1024)S(1)}, f32[3072]{0:T(1024)}, u32[]{:S(2)}) copy-start(f32[3072]{0:T(1024)} %param.41) | copy-start | bytes 36868
  285.9 31.2 %copy-start.21 = (f32[8,768]{1,0:T(8,128)S(1)}, f32[8,768]{1,0:T(8,128)}, u32[]{:S(2)}) copy-start(f32[8,768]{1,0:T(8,128)} %get-tuple-element.78) | copy-start | bytes 73732
  285.9 33.1 %copy-start.22 = (f32[2,1,768]{2,1,0:T(1,128)S(1)}, f32[2,1,768]{2,1,0:T(1,128)}, u32[]{:S(2)}) copy-start(f32[2,1,768]{2,1,0:T(1,128)} %get-tuple-element.80) | copy-start | bytes 18436
  320.1 122.1 %copy-start.9 = (f32[96,3,192]{2,0,1:T(8,128)S(1)}, f32[96,3,192]{2,0,1:T(8,128)}, u32[]{:S(2)}) copy-start(f32[96,3,192]{2,0,1:T(8,128)} %param.27) | copy-start | bytes 663556
  436.9 5.5 %copy-start.10 = (f32[96,3,192]{2,0,1:T(8,128)S(1)}, f32[96,3,192]{2,0,1:T(8,128)}, u32[]{:S(2)}) copy-start(f32[96,3,192]{2,0,1:T(8,128)} %param.28) | copy-start | bytes 663556
  442.4 3.1 copy-start.14
  442.4 4.1 copy-start.12
  442.6 6.3 %copy-start.6 = (f32[96,768]{1,0:T(8,128)S(1)}, f32[96,768]{1,0:T(8,128)}, u32[]{:S(2)}) copy-start(f32[96,768]{1,0:T(8,128)} %param.33) | copy-start | bytes 884740
  442.6 6.3 %copy-start.8 = (f32[96,768]{1,0:T(8,128)S(1)}, f32[96,768]{1,0:T(8,128)}, u32[]{:S(2)}) copy-start(f32[96,768]{1,0:T(8,128)} %get-tuple-element.85) | copy-start | bytes 884740
  442.8 6.1 %copy-start.7 = (f32[96,768]{1,0:T(8,128)S(1)}, f32[96,768]{1,0:T(8,128)}, u32[]{:S(2)}) copy-start(f32[96,768]{1,0:T(8,128)} %param.34) | copy-start | bytes 884740
  446.6 5.6 %copy-start.5 = (f32[8,768]{1,0:T(8,128)S(1)}, f32[8,768]{1,0:T(8,128)}, u32[]{:S(2)}) copy-start(f32[8,768]{1,0:T(8,128)} %vec_ref.7) | copy-start | bytes 73732
  446.7 5.6 %copy-start.11 = (f32[16,768]{1,0:T(8,128)S(1)}, f32[16,768]{1,0:T(8,128)}, u32[]{:S(2)}) copy-start(f32[16,768]{1,0:T(8,128)} %get-tuple-element.82) | copy-start | bytes 147460
  446.7 5.6 %copy-start.16 = (f32[8,768]{1,0:T(8,128)S(1)}, f32[8,768]{1,0:T(8,128)}, u32[]{:S(2)}) copy-start(f32[8,768]{1,0:T(8,128)} %param.39) | copy-start | bytes 73732
  446.7 5.6 %copy-start.17 = (f32[8,768]{1,0:T(8,128)S(1)}, f32[8,768]{1,0:T(8,128)}, u32[]{:S(2)}) copy-start(f32[8,768]{1,0:T(8,128)} %param.40) | copy-start | bytes 73732
  447.4 5.5 %copy-start.19 = (f32[3072]{0:T(1024)S(1)}, f32[3072]{0:T(1024)}, u32[]{:S(2)}) copy-start(f32[3072]{0:T(1024)} %param.42) | copy-start | bytes 36868
  447.4 5.5 %copy-start.20 = (f32[3072]{0:T(1024)S(1)}, f32[3072]{0:T(1024)}, u32[]{:S(2)}) copy-start(f32[3072]{0:T(1024)} %param.43) | copy-start | bytes 36868
  448.2 5.4 %copy-start.2 = (bf16[768,768]{1,0:T(8,128)(2,1)S(1)}, bf16[768,768]{1,0:T(8,128)(2,1)}, u32[]{:S(2)}) copy-start(bf16[768,768]{1,0:T(8,128)(2,1)} %get-tuple-element.209) | copy-start | bytes 3538948
  450.0 4.6 %copy-start.3 = (bf16[768,768]{1,0:T(8,128)(2,1)S(1)}, bf16[768,768]{1,0:T(8,128)(2,1)}, u32[]{:S(2)}) copy-start(bf16[768,768]{1,0:T(8,128)(2,1)} %get-tuple-element.210) | copy-start | bytes 3538948
